TPU v7x, 32 devices: a whole 2x2x4 slice. The times are simulated.
32 devices in a mesh: dp: 8 (over z, x), seq: 4 (over y, core).
Axes of the slice: x: 2, y: 2, z: 4, core: 2. Of those that a mesh axis runs over, the one named last changes fastest.
Arguments:
- tokens: bfloat16 [16, 1024, 1024], P('dp', 'seq'), may hold values from -6 to 6
- cotangent: bfloat16 [16, 1024, 1024], P('dp', 'seq'), may hold values from -6 to 6
- src_len: int32 [16], P('dp'), may hold values from 30 to 400
- tgt_len: int32 [16], P('dp'), may hold values from 1 to 994, as said below
- attn_gain: bfloat16 [1024], replicated, may hold values from 0.5 to 1.5
- attn_shift: bfloat16 [1024], replicated, may hold values from -1.75 to 1.75
- qkv_weight: bfloat16 [1024, 3072], replicated, may hold values from -0.1875 to 0.1875
- qkv_bias: bfloat16 [3072], replicated, may hold values from -1.75 to 1.75
- out_weight: bfloat16 [1024, 1024], replicated, may hold values from -1.5 to 1.5
- out_bias: bfloat16 [1024], replicated, may hold values from -1.75 to 1.75
- mlp_gain: bfloat16 [1024], replicated, may hold values from 0.099609375 to 1.8984375
- mlp_shift: bfloat16 [1024], replicated, may hold values from -1.75 to 1.75
- fc_weight: bfloat16 [1024, 4096], replicated, may hold values from -0.1875 to 0.1875
- fc_bias: bfloat16 [4096], replicated, may hold values from -1.75 to 1.75
- proj_weight: bfloat16 [4096, 1024], replicated, may hold values from -0.125 to 0.125
- proj_bias: bfloat16 [1024], replicated, may hold values from -1.75 to 1.75
- embed_rows: bfloat16 [10, 1024], replicated, may hold values from -6 to 6
- mid_weight: bfloat16 [1024, 512], replicated, may hold values from -0.1875 to 0.1875
- mid_bias: bfloat16 [512], replicated, may hold values from -3 to 3
- kv_weight: bfloat16 [512, 2048], replicated, may hold values from -0.5 to 0.5
- kv_bias: bfloat16 [2048], replicated, may hold values from -3 to 3
Outputs:
- hidden_out: bfloat16 [16, 1024, 1024], P('dp', 'seq')
- grad_tokens: bfloat16 [16, 1024, 1024], P('dp', 'seq')
- grad_embed: float32 [10, 1024], replicated
- grad_midw: float32 [1024, 512], replicated
- grad_midb: float32 [512], replicated
- grad_kvw: float32 [512, 2048], replicated
- grad_kvb: float32 [2048], replicated
Inputs may be any that keep to these rules, and one draw needn't show every extreme that they name: src_len + tgt_len <= 1024; in every aligned block of 2 rows one row has src_len + tgt_len = 1024.
All inputs are finite; a program needn't handle non-finite values.
Results may differ from a plain program's by a relative error of at most 0.015.
Values may be sent and summed in bfloat16 or wider, within the bound.
A program may use at most 256 MiB of HBM per device.

v0:
```python
import jax
import jax.numpy as jnp
from jax import lax
from jax.sharding import PartitionSpec as P

HEADS = 16
HD = 64


EPS = 1e-05
NEG = -1e30
HIGH = lax.Precision.HIGHEST


def layer_norm(values_in, gain_vec, shift_vec):
    mean_row = jnp.mean(values_in, axis=-1, keepdims=True)
    centered = values_in - mean_row
    var_row = jnp.mean(centered * centered, axis=-1, keepdims=True)
    return centered * lax.rsqrt(var_row + EPS) * gain_vec + shift_vec


def gelu_tanh(values_in):
    return jax.nn.gelu(values_in, approximate=True)


def paired(array_in):
    return array_in.reshape((array_in.shape[0] // 2, 2) + array_in.shape[1:])


def unpaired(array_in):
    return array_in.reshape((array_in.shape[0] * 2,) + array_in.shape[2:])


def heads_of(array_in):
    return array_in.reshape(array_in.shape[:-1] + (HEADS, array_in.shape[-1] // HEADS))


def causal_allowed(query_pos, key_pos, lengths):
    allowed = (key_pos[None, None, :] <= query_pos[None, :, None]) & (
        key_pos[None, None, :] < lengths[:, None, None]
    )
    return allowed[:, None]


def head_scores(queries, keys_all, prefix_keys):
    token_scores = jnp.einsum(
        "gqhe,gkhe->ghqk", queries, keys_all, preferred_element_type=jnp.float32
    )
    prefix_scores = jnp.einsum(
        "gqhe,khe->ghqk", queries, prefix_keys, preferred_element_type=jnp.float32
    )
    return (prefix_scores, token_scores)


def forward_group(pieces, prefix_keys, prefix_vals, offset):
    queries, keys_all, vals_all, lengths = pieces
    query_pos = offset + jnp.arange(queries.shape[1], dtype=jnp.int32)
    key_pos = jnp.arange(keys_all.shape[1], dtype=jnp.int32)
    prefix_scores, token_scores = head_scores(queries, keys_all, prefix_keys)
    token_scores = jnp.where(causal_allowed(query_pos, key_pos, lengths), token_scores, NEG)
    maxima = jnp.maximum(jnp.max(prefix_scores, axis=-1), jnp.max(token_scores, axis=-1))
    prefix_exp = jnp.exp(prefix_scores - maxima[..., None])
    token_exp = jnp.exp(token_scores - maxima[..., None])
    denoms = jnp.sum(prefix_exp, axis=-1) + jnp.sum(token_exp, axis=-1)
    prefix_pb = (prefix_exp / denoms[..., None]).astype(jnp.bfloat16)
    token_pb = (token_exp / denoms[..., None]).astype(jnp.bfloat16)
    attended = jnp.einsum("ghqk,gkhe->gqhe", token_pb, vals_all, preferred_element_type=jnp.float32)
    attended = attended + jnp.einsum(
        "ghqk,khe->gqhe", prefix_pb, prefix_vals, preferred_element_type=jnp.float32
    )
    return (attended, maxima, denoms)


def query_back(pieces, prefix_keys, prefix_vals, offset):
    queries, keys_all, vals_all, lengths, grad_heads, maxima, denoms = pieces
    query_pos = offset + jnp.arange(queries.shape[1], dtype=jnp.int32)
    key_pos = jnp.arange(keys_all.shape[1], dtype=jnp.int32)
    prefix_scores, token_scores = head_scores(queries, keys_all, prefix_keys)
    token_scores = jnp.where(causal_allowed(query_pos, key_pos, lengths), token_scores, NEG)
    prefix_probs = jnp.exp(prefix_scores - maxima[..., None]) / denoms[..., None]
    token_probs = jnp.exp(token_scores - maxima[..., None]) / denoms[..., None]
    token_dprob = jnp.einsum(
        "gqhe,gkhe->ghqk", grad_heads, vals_all, preferred_element_type=jnp.float32
    )
    prefix_dprob = jnp.einsum(
        "gqhe,khe->ghqk", grad_heads, prefix_vals, preferred_element_type=jnp.float32
    )
    delta_rows = jnp.sum(prefix_probs * prefix_dprob, axis=-1) + jnp.sum(
        token_probs * token_dprob, axis=-1
    )
    token_ds = (token_probs * (token_dprob - delta_rows[..., None])).astype(jnp.bfloat16)
    prefix_ds = (prefix_probs * (prefix_dprob - delta_rows[..., None])).astype(jnp.bfloat16)
    grad_query = jnp.einsum(
        "ghqk,gkhe->gqhe", token_ds, keys_all, preferred_element_type=jnp.float32
    )
    grad_query = (
        grad_query
        + jnp.einsum("ghqk,khe->gqhe", prefix_ds, prefix_keys, preferred_element_type=jnp.float32)
    ) * HD ** (-0.5)
    grad_pkey = jnp.einsum("ghqk,gqhe->khe", prefix_ds, queries, preferred_element_type=jnp.float32)
    grad_pval = jnp.einsum(
        "ghqk,gqhe->khe",
        prefix_probs.astype(jnp.bfloat16),
        grad_heads,
        preferred_element_type=jnp.float32,
    )
    grad_key = jnp.einsum("ghqk,gqhe->gkhe", token_ds, queries, preferred_element_type=jnp.float32)
    grad_val = jnp.einsum(
        "ghqk,gqhe->gkhe",
        token_probs.astype(jnp.bfloat16),
        grad_heads,
        preferred_element_type=jnp.float32,
    )
    return (grad_query, grad_pkey, grad_pval, delta_rows, grad_key, grad_val)


def reparam_back(grad_prefix, embed_f, midw_f, kvw_f, prefix_hidden):
    grad_kvb = jnp.sum(grad_prefix, axis=0)
    grad_kvw = jnp.dot(prefix_hidden.T, grad_prefix, precision=HIGH)
    grad_pre = jnp.dot(grad_prefix, kvw_f.T, precision=HIGH) * (1.0 - prefix_hidden * prefix_hidden)
    grad_midb = jnp.sum(grad_pre, axis=0)
    grad_midw = jnp.dot(embed_f.T, grad_pre, precision=HIGH)
    grad_embed = jnp.dot(grad_pre, midw_f.T, precision=HIGH)
    return (grad_embed, grad_midw, grad_midb, grad_kvw, grad_kvb)


def on_device(
    tokens,
    cotangent,
    src_len,
    tgt_len,
    attn_gain,
    attn_shift,
    qkv_weight,
    qkv_bias,
    out_weight,
    out_bias,
    mlp_gain,
    mlp_shift,
    fc_weight,
    fc_bias,
    proj_weight,
    proj_bias,
    embed_rows,
    mid_weight,
    mid_bias,
    kv_weight,
    kv_bias,
):
    rows_dev, seg_len, width = tokens.shape
    offset = lax.axis_index("seq") * seg_len
    totals = src_len + tgt_len
    embed_f = embed_rows.astype(jnp.float32)
    midw_f = mid_weight.astype(jnp.float32)
    kvw_f = kv_weight.astype(jnp.float32)
    prefix_hidden = jnp.tanh(
        jnp.dot(embed_f, midw_f, precision=HIGH) + mid_bias.astype(jnp.float32)
    )
    prefix_kv = jnp.dot(prefix_hidden, kvw_f, precision=HIGH) + kv_bias.astype(jnp.float32)
    prefix_keys = heads_of(prefix_kv[:, :width].astype(jnp.bfloat16))
    prefix_vals = heads_of(prefix_kv[:, width:].astype(jnp.bfloat16))
    inputs_f = tokens.astype(jnp.float32)

    def norm_attn(values_in):
        return layer_norm(values_in, attn_gain.astype(jnp.float32), attn_shift.astype(jnp.float32))

    normed_one, pull_one = jax.vjp(norm_attn, inputs_f)
    mixed_qkv = jnp.einsum(
        "rld,de->rle",
        normed_one.astype(jnp.bfloat16),
        qkv_weight,
        preferred_element_type=jnp.float32,
    )
    mixed_qkv = (mixed_qkv + qkv_bias.astype(jnp.float32)).astype(jnp.bfloat16)
    queries = heads_of(mixed_qkv[..., :width] * HD ** (-0.5))
    keys_loc = mixed_qkv[..., width : 2 * width]
    vals_loc = mixed_qkv[..., 2 * width :]
    keys_all, vals_all = (
        lax.all_gather(keys_loc, "seq", axis=1, tiled=True),
        lax.all_gather(vals_loc, "seq", axis=1, tiled=True),
    )
    keys_all = heads_of(keys_all)
    vals_all = heads_of(vals_all)

    def attend_pair(pieces):
        return forward_group(pieces, prefix_keys, prefix_vals, offset)

    attended, maxima, denoms = lax.map(
        attend_pair, (paired(queries), paired(keys_all), paired(vals_all), paired(totals))
    )
    attended = unpaired(attended).reshape(rows_dev, seg_len, width).astype(jnp.bfloat16)
    maxima = unpaired(maxima)
    denoms = unpaired(denoms)
    middle = (
        inputs_f
        + jnp.einsum("rld,de->rle", attended, out_weight, preferred_element_type=jnp.float32)
        + out_bias.astype(jnp.float32)
    )

    def norm_mlp(values_in):
        return layer_norm(values_in, mlp_gain.astype(jnp.float32), mlp_shift.astype(jnp.float32))

    normed_two, pull_two = jax.vjp(norm_mlp, middle)
    upward = jnp.einsum(
        "rld,df->rlf",
        normed_two.astype(jnp.bfloat16),
        fc_weight,
        preferred_element_type=jnp.float32,
    ) + fc_bias.astype(jnp.float32)
    active, pull_gelu = jax.vjp(gelu_tanh, upward)
    hidden_out = middle + jnp.einsum(
        "rlf,fd->rld", active.astype(jnp.bfloat16), proj_weight, preferred_element_type=jnp.float32
    )
    hidden_out = (hidden_out + proj_bias.astype(jnp.float32)).astype(jnp.bfloat16)
    positions = offset + jnp.arange(seg_len, dtype=jnp.int32)
    target = (positions[None, :] >= src_len[:, None]) & (positions[None, :] < totals[:, None])
    grad_seed = cotangent * target[:, :, None].astype(jnp.bfloat16)
    grad_active = jnp.einsum(
        "rld,fd->rlf", grad_seed, proj_weight, preferred_element_type=jnp.float32
    )
    grad_up = pull_gelu(grad_active)[0].astype(jnp.bfloat16)
    grad_normed = jnp.einsum("rlf,df->rld", grad_up, fc_weight, preferred_element_type=jnp.float32)
    grad_middle = grad_seed.astype(jnp.float32) + pull_two(grad_normed)[0]
    grad_att = jnp.einsum(
        "rle,de->rld",
        grad_middle.astype(jnp.bfloat16),
        out_weight,
        preferred_element_type=jnp.float32,
    ).astype(jnp.bfloat16)
    grad_heads = heads_of(grad_att)

    def back_pair(pieces):
        return query_back(pieces, prefix_keys, prefix_vals, offset)

    results = lax.map(
        back_pair,
        (
            paired(queries),
            paired(keys_all),
            paired(vals_all),
            paired(totals),
            paired(grad_heads),
            paired(maxima),
            paired(denoms),
        ),
    )
    grad_query = unpaired(results[0]).reshape(rows_dev, seg_len, width)
    grad_pkey = jnp.sum(results[1], axis=0).reshape(-1, width)
    grad_pval = jnp.sum(results[2], axis=0).reshape(-1, width)
    key_terms = unpaired(results[4]).reshape(rows_dev, -1, width)
    val_terms = unpaired(results[5]).reshape(rows_dev, -1, width)
    grad_key, grad_val = (
        lax.psum_scatter(
            key_terms.astype(jnp.bfloat16), "seq", scatter_dimension=1, tiled=True
        ).astype(jnp.float32),
        lax.psum_scatter(
            val_terms.astype(jnp.bfloat16), "seq", scatter_dimension=1, tiled=True
        ).astype(jnp.float32),
    )
    grad_mixed = jnp.concatenate([grad_query, grad_key, grad_val], axis=-1).astype(jnp.bfloat16)
    grad_normed_one = jnp.einsum(
        "rle,de->rld", grad_mixed, qkv_weight, preferred_element_type=jnp.float32
    )
    grad_tokens = (grad_middle + pull_one(grad_normed_one)[0]).astype(jnp.bfloat16)
    grad_prefix = jnp.concatenate([grad_pkey, grad_pval], axis=-1)
    grad_embed, grad_midw, grad_midb, grad_kvw, grad_kvb = reparam_back(
        grad_prefix, embed_f, midw_f, kvw_f, prefix_hidden
    )
    grad_embed, grad_midw, grad_midb, grad_kvw, grad_kvb = lax.psum(
        (grad_embed, grad_midw, grad_midb, grad_kvw, grad_kvb), ("dp", "seq")
    )
    return (hidden_out, grad_tokens, grad_embed, grad_midw, grad_midb, grad_kvw, grad_kvb)


def solution(mesh):
    placed = (
        P("dp", "seq", None),
        P("dp", "seq", None),
        P("dp"),
        P("dp"),
        P(),
        P(),
        P(),
        P(),
        P(),
        P(),
        P(),
        P(),
        P(),
        P(),
        P(),
        P(),
        P(),
        P(),
        P(),
        P(),
        P(),
    )
    return jax.shard_map(
        on_device,
        mesh=mesh,
        in_specs=placed,
        out_specs=(P("dp", "seq", None), P("dp", "seq", None), P(), P(), P(), P(), P()),
        check_vma=False,
    )
```

profile of v0, /device:TPU:0, one launch (start us, length us, event | category | flops | bytes accessed | tf_op | source)
XLA Modules:
  0.0 473.4 jit_solution(10938268272671504178)
XLA Ops:
  7.2 1.6 convert_reduce_fusion
  8.8 1.6 fusion.47
  10.5 0.7 convert_element_type.124
  11.2 0.7 convert_element_type.125
  11.9 0.7 convert_element_type.127
  12.6 6.7 %add_convert_fusion = bf16[2,256,3072]{2,1,0:T(8,128)(2,1)S(1)} fusion(bf16[1024,3072]{1,0:T(8,128)(2,1)} %param.27, f32[3072]{0:T(1024)S(1)} %convert_element_type.127, bf16[2,256,1024]{2,1,0:T(8,128)(2,1)} %param.21, f32[1024]{0:T(1024)S(1)} %convert_element_type.125, f32[1024]{0:T(1024)S(1)} %convert_element_type.124, f32[2,256]{1,0:T(2,128)S(1)} %fusion.102, ...), kind=kOutput, calls=%fused_computation.32 | convolution fusion | flops 3227516928 | bytes 10510336 | tf_op jit(solution)/shard_map/rld,de->rle/dot_general | solution.py:168
  19.3 1.7 fusion.113
  21.2 0.7 all-gather.3.cloned.1.call-update
  22.1 0.3 fusion.70
  22.3 0.6 copy-done.21
  22.9 2.5 fusion.46
  25.7 1.9 copy.130
  28.1 1.1 broadcast_and_fusion
  29.1 1.1 fusion.115
  30.2 28.2 %all-gather.5.cloned.1.call-done = bf16[2,1024,1024]{2,1,0:T(8,128)(2,1)} async-done(((bf16[2,256,1024]{2,1,0:T(8,128)(2,1)}), bf16[2,1024,1024]{2,1,0:T(8,128)(2,1)}) %all-gather.5.cloned.1.call-update) | async-done | bytes 4194320 | tf_op jit(solution)/shard_map/all_gather | solution.py:179
  58.4 6.2 %copy.131 = bf16[2,1024,1024]{1,2,0:T(8,128)(2,1)} copy(bf16[2,1024,1024]{2,1,0:T(8,128)(2,1)} %all-gather.5.cloned.1.call-done) | data formatting | bytes 8388608 | tf_op jit(solution)/shard_map/all_gather | solution.py:179
  64.7 16.1 %select_reduce_fusion = (f32[2,16,256]{2,1,0:T(8,128)S(1)}, f32[2,16,256,1024]{3,2,1,0:T(8,128)}) fusion(pred[2,256,1024]{2,1,0:T(8,128)(4,1)} %broadcast_and_fusion, bf16[2,256,16,64]{1,3,2,0:T(8,128)(2,1)S(1)} %bitcast.113, bf16[2,1024,16,64]{1,3,2,0:T(8,128)(2,1)} %bitcast.110), kind=kOutput, calls=%fused_computation.3 | convolution fusion | flops 1090510848 | bytes 39354368 | tf_op jit(solution)/shard_map/while/body/eval_jaxpr/gqhe,gkhe->ghqk/dot_general | solution.py:46
  81.0 14.6 %fusion.1 = f32[2,16,256]{2,1,0:T(8,128)S(1)} fusion(f32[2,16,256,1024]{3,2,1,0:T(8,128)} %get-tuple-element.136, f32[2,16,256]{2,1,0:T(8,128)S(1)} %copy_maximum_fusion, pred[2,256,1024]{2,1,0:T(8,128)(4,1)S(1)} %copy-done.8), kind=kLoop, calls=%fused_computation.5 | loop fusion | flops 25157632 | bytes 34144256 | tf_op jit(solution)/shard_map/while/body/eval_jaxpr/reduce_sum | solution.py:64
  95.7 1.8 fusion.94
  97.6 6.2 %copy.129 = bf16[2,1024,1024]{1,2,0:T(8,128)(2,1)} copy(bf16[2,1024,1024]{2,1,0:T(8,128)(2,1)} %all-gather.3.cloned.1.call-done) | data formatting | bytes 8388608 | tf_op jit(solution)/shard_map/all_gather | solution.py:180
  103.8 15.7 %fusion.59 = bf16[2,256,16,64]{1,3,2,0:T(8,128)(2,1)S(1)} fusion(f32[16,64,2,256]{3,1,0,2:T(8,128)} %fusion.94, bf16[2,1024,16,64]{1,3,2,0:T(8,128)(2,1)} %bitcast.117, f32[2,16,256,1024]{3,2,1,0:T(8,128)} %get-tuple-element.136, f32[2,16,256]{2,1,0:T(8,128)S(1)} %copy_add_fusion.1, f32[2,16,256]{2,1,0:T(8,128)S(1)} %copy_maximum_fusion, ...), kind=kOutput, calls=%fused_computation.70 | convolution fusion | flops 1108344832 | bytes 41484288 | tf_op jit(solution)/shard_map/while/body/eval_jaxpr/ghqk,gkhe->gqhe/dot_general | solution.py:67
  119.5 1.4 fusion.116
  121.0 0.3 multiply_reduce_fusion.2
  121.3 10.7 %fusion.15 = f32[2,256,4096]{2,1,0:T(8,128)} fusion(bf16[1024,4096]{1,0:T(8,128)(2,1)} %param.33, f32[2,256,1024]{2,1,0:T(8,128)S(1)} %get-tuple-element.140, f32[1024]{0:T(1024)S(1)} %convert_element_type.137, f32[1024]{0:T(1024)S(1)} %convert_element_type.136, f32[2,256]{1,0:T(2,128)S(1)} %fusion.103, f32[2,256]{1,0:T(2,128)S(1)} %broadcast_multiply_fusion), kind=kOutput, calls=%fused_computation.21 | convolution fusion | flops 4297588736 | bytes 18886656 | tf_op jit(solution)/shard_map/rld,df->rlf/dot_general | solution.py:204
  132.0 15.5 %fusion.8 = bf16[2,256,4096]{2,1,0:T(8,128)(2,1)} fusion(f32[2,256,4096]{2,1,0:T(8,128)} %fusion.15, bf16[4096,1024]{1,0:T(8,128)(2,1)} %param.35, f32[4096]{0:T(1024)S(1)} %convert_element_type.139, bf16[2,256,1024]{2,1,0:T(8,128)(2,1)S(1)} %copy-done.17, bf16[2,256]{1,0:T(2,128)(2,1)S(1)} %and_convert_fusion), kind=kOutput, calls=%fused_computation.14 | convolution fusion | flops 4339531776 | bytes 22037504 | tf_op jit(solution)/shard_map/rld,fd->rlf/dot_general | solution.py:218
  147.5 6.7 %multiply_reduce_fusion.1 = (f32[2,256]{1,0:T(2,128)S(1)}, f32[2,256,1024]{2,1,0:T(8,128)S(1)}) fusion(f32[2,256,1024]{2,1,0:T(8,128)S(1)} %get-tuple-element.140, f32[1024]{0:T(1024)S(1)} %convert_element_type.136, f32[2,256]{1,0:T(2,128)S(1)} %broadcast_multiply_fusion, bf16[2,256,4096]{2,1,0:T(8,128)(2,1)} %fusion.8, bf16[1024,4096]{1,0:T(8,128)(2,1)S(1)} %bitcast.129), kind=kOutput, calls=%fused_computation.73 | convolution fusion | flops 4297063936 | bytes 16785408 | tf_op jit(solution)/shard_map/rlf,df->rld/dot_general | solution.py:222
  154.2 0.7 fusion.112
  154.9 1.3 copy-done.10
  156.2 2.3 fusion.64
  158.5 1.5 copy.141
  160.0 0.4 convolution_bitcast_fusion.3
  160.4 26.6 %multiply_reduce_fusion = (f32[2,16,256]{2,1,0:T(8,128)S(1)}, f32[2,16,256,1024]{3,2,1,0:T(8,128)}) fusion(f32[2,16,256]{2,1,0:T(8,128)S(1)} %copy_add_fusion.1, f32[2,16,256]{2,1,0:T(8,128)S(1)} %copy_maximum_fusion, f32[2,16,256,1024]{3,2,1,0:T(8,128)} %get-tuple-element.136, pred[2,256,1024]{2,1,0:T(8,128)(4,1)S(1)} %copy-done.9, ...), kind=kOutput, calls=%fused_computation.1 | convolution fusion | flops 1115676672 | bytes 72974336 | tf_op jit(solution)/shard_map/while/body/eval_jaxpr/gqhe,gkhe->ghqk/dot_general | solution.py:82
  187.1 0.7 reshape.244
  187.8 0.3 multiply_reduce_fusion.3
  188.2 0.6 copy-done.26
  189.0 0.4 convolution_bitcast_fusion.4
  189.5 0.8 constant_dynamic-update-slice_fusion
  190.3 3.9 fusion.117
  194.3 5.8 %fusion.120 = f32[512,2048]{1,0:T(8,128)} fusion(f32[10,512]{1,0:T(8,128)} %copy-done.21, f32[10,2048]{1,0:T(8,128)S(1)} %constant_dynamic-update-slice_fusion), kind=kOutput, calls=%fused_computation.154 | convolution fusion | flops 125829120 | bytes 4296704 | tf_op jit(solution)/shard_map/dot_general | solution.py:119
  200.0 2.4 convolution_bitcast_fusion
  202.5 15.9 %fusion.43 = bf16[2,16,64,1024]{3,2,1,0:T(8,128)(2,1)} fusion(bf16[2,256,16,64]{1,3,2,0:T(8,128)(2,1)S(1)} %bitcast.124, f32[2,16,256,1024]{3,2,1,0:T(8,128)} %get-tuple-element.136, f32[2,16,256]{2,1,0:T(8,128)S(1)} %copy-done.25, f32[2,16,256]{2,1,0:T(8,128)S(1)} %copy-done.23, pred[2,256,1024]{2,1,0:T(8,128)(4,1)S(1)} %copy-done.9), kind=kOutput, calls=%fused_computation.53 | convolution fusion | flops 1109393408 | bytes 39387136 | tf_op jit(solution)/shard_map/while/body/eval_jaxpr/ghqk,gqhe->gkhe/dot_general | solution.py:108
  218.4 6.3 %copy.149 = bf16[2,1024,1024]{2,1,0:T(8,128)(2,1)} copy(bf16[2,1024,1024]{1,2,0:T(8,128)(2,1)} %bitcast.119) | data formatting | bytes 8388608 | tf_op jit(solution)/shard_map/convert_element_type | solution.py:257
  224.8 0.7 copy-done.27
  225.5 29.0 %multiply_convert_fusion = bf16[2,16,256,1024]{3,2,1,0:T(8,128)(2,1)} fusion(f32[2,16,256,1024]{3,2,1,0:T(8,128)} %get-tuple-element.144, f32[2,16,256]{2,1,0:T(8,128)S(1)} %copy-done.27, f32[2,16,256]{2,1,0:T(8,128)S(1)} %copy-done.25, f32[2,16,256]{2,1,0:T(8,128)S(1)} %copy-done.23, f32[2,16,256,1024]{3,2,1,0:T(8,128)} %get-tuple-element.136, ...), kind=kLoop, calls=%fused_computation | loop fusion | flops 50331648 | bytes 84508672 | tf_op jit(solution)/shard_map/while/body/eval_jaxpr/convert_element_type | solution.py:91
  254.5 11.0 %convolution_convert_fusion = bf16[2,16,64,1024]{3,2,1,0:T(8,128)(2,1)} fusion(bf16[2,256,16,64]{1,3,2,0:T(8,128)(2,1)S(1)} %bitcast.115, bf16[2,16,256,1024]{3,2,1,0:T(8,128)(2,1)} %multiply_convert_fusion), kind=kOutput, calls=%fused_computation.52 | convolution fusion | flops 1075838976 | bytes 22020096 | tf_op jit(solution)/shard_map/while/body/eval_jaxpr/ghqk,gqhe->gkhe/dot_general | solution.py:107
  265.6 6.2 %copy.148 = bf16[2,1024,1024]{2,1,0:T(8,128)(2,1)} copy(bf16[2,1024,1024]{1,2,0:T(8,128)(2,1)} %bitcast.116) | data formatting | bytes 8388608 | tf_op jit(solution)/shard_map/convert_element_type | solution.py:254
  271.8 0.7 copy-done.52
  272.4 0.6 convert_element_type.141
  273.0 13.7 %fusion.118 = f32[2,16,64,256]{3,2,1,0:T(8,128)} fusion(bf16[2,1024,16,64]{1,3,2,0:T(8,128)(2,1)} %bitcast.111, bf16[2,16,256,1024]{3,2,1,0:T(8,128)(2,1)} %multiply_convert_fusion), kind=kOutput, calls=%fused_computation.152 | convolution fusion | flops 1073741824 | bytes 23068672 | tf_op jit(solution)/shard_map/while/body/eval_jaxpr/ghqk,gkhe->gqhe/dot_general | solution.py:93
  286.7 3.2 fusion.54
  290.0 2.3 copy.150
  292.3 1.7 fusion.119
  294.0 42.1 %all-reduce = (f32[10,1024]{1,0:T(8,128)}, f32[512]{0:T(512)}, f32[2048]{0:T(1024)}) all-reduce(f32[10,1024]{1,0:T(8,128)S(1)} %fusion.119, f32[512]{0:T(512)} %get-tuple-element.149, f32[2048]{0:T(1024)S(1)} %reduce_sum.167), channel_id=1, replica_groups=mesh['dp'=8,'seq'=4] {'dp','seq'}, use_global_device_ids=true, to_apply=%region_16.17 | all-reduce | flops 12800 | bytes 102400 | tf_op jit(solution)/shard_map/psum | solution.py:269
  336.1 12.6 %add_convert_fusion.2 = bf16[2,256,1024]{2,1,0:T(8,128)(2,1)} fusion(f32[2,256,1024]{2,1,0:T(8,128)S(1)} %copy-done.7, bf16[4096,1024]{1,0:T(8,128)(2,1)} %param.35, f32[2,256,4096]{2,1,0:T(8,128)} %fusion.15, f32[4096]{0:T(1024)S(1)} %copy-done.42, f32[1024]{0:T(1024)} %convert_element_type.141), kind=kOutput, calls=%fused_computation.74 | convolution fusion | flops 4317511680 | bytes 19943424 | tf_op jit(solution)/shard_map/rlf,fd->rld/dot_general | solution.py:211
  348.7 10.8 %all-reduce.4.cloned.1.call-done = (f32[1024,512]{0,1:T(8,128)}, f32[512,2048]{1,0:T(8,128)}) async-done(((f32[1024,512]{0,1:T(8,128)}, f32[512,2048]{1,0:T(8,128)}), (f32[1024,512]{0,1:T(8,128)}, f32[512,2048]{1,0:T(8,128)})) %all-reduce.4.cloned.1.call-update) | async-done | bytes 6291472 | tf_op jit(solution)/shard_map/psum | solution.py:269
  359.5 2.9 copy.155
  362.4 43.7 %reduce-scatter.5.cloned.1.call-done = bf16[2,256,1024]{2,1,0:T(8,128)(2,1)} async-done(((bf16[2,1024,1024]{2,1,0:T(8,128)(2,1)}), bf16[2,256,1024]{2,1,0:T(8,128)(2,1)}) %reduce-scatter.5.cloned.1.call-update) | async-done | bytes 1048592 | tf_op jit(solution)/shard_map/reduce_scatter | solution.py:256
  406.1 46.9 %reduce-scatter.3.cloned.1.call-done = bf16[2,256,1024]{2,1,0:T(8,128)(2,1)} async-done(((bf16[2,1024,1024]{2,1,0:T(8,128)(2,1)}), bf16[2,256,1024]{2,1,0:T(8,128)(2,1)}) %reduce-scatter.3.cloned.1.call-update) | async-done | bytes 1048592 | tf_op jit(solution)/shard_map/reduce_scatter | solution.py:253
  453.1 7.0 %fusion.51 = (f32[2,256]{1,0:T(2,128)S(1)}, f32[2,256,1024]{2,1,0:T(8,128)S(1)}) fusion(bf16[2,256,1024]{2,1,0:T(8,128)(2,1)S(1)} %copy-done.5, f32[1024]{0:T(1024)S(1)} %copy-done.34, f32[2,256]{1,0:T(2,128)S(1)} %copy-done.36, bf16[1024,3072]{1,0:T(8,128)(2,1)} %param.27, bf16[2,256,1024]{2,1,0:T(8,128)(2,1)} %reduce-scatter.5.cloned.1.call-done, ...), kind=kOutput, calls=%fused_computation.60 | convolution fusion | flops 3233283584 | bytes 12591104 | tf_op jit(solution)/shard_map/rle,de->rld/dot_general | solution.py:261
  460.1 0.7 fusion.84
  460.9 0.8 copy-done.11
  461.7 1.9 add_convert_fusion.1
  463.6 2.1 copy.201
  465.7 1.0 copy-done.1
  (155 shorter events, 1.9 us)
Async XLA Ops:
  7.2 112.4 %copy-start = (bf16[1024,1024]{1,0:T(8,128)(2,1)S(1)}, bf16[1024,1024]{1,0:T(8,128)(2,1)}, u32[]{:S(2)}) copy-start(bf16[1024,1024]{1,0:T(8,128)(2,1)} %param.29) | copy-start | bytes 6291460
  7.2 51.3 %all-gather.5.cloned.1.call-start = ((), (), s32[]{:S(2)}) async-start(), calls=%async_computation.3 | async-start | bytes 5242880 | tf_op jit(solution)/shard_map/all_gather | solution.py:179
  8.8 10.4 %copy-start.35 = (f32[2,256]{1,0:T(2,128)}, f32[2,256]{1,0:T(2,128)S(1)}, u32[]{:S(2)}) copy-start(f32[2,256]{1,0:T(2,128)S(1)} %broadcast_multiply_fusion.1) | copy-start | bytes 6148
  10.5 1.4 copy-start.39
  10.5 8.8 %copy-start.37 = (f32[2,256]{1,0:T(2,128)}, f32[2,256]{1,0:T(2,128)S(1)}, u32[]{:S(2)}) copy-start(f32[2,256]{1,0:T(2,128)S(1)} %fusion.102) | copy-start | bytes 6148
  11.2 8.1 %copy-start.33 = (f32[1024]{0:T(1024)}, f32[1024]{0:T(1024)S(1)}, u32[]{:S(2)}) copy-start(f32[1024]{0:T(1024)S(1)} %convert_element_type.124) | copy-start | bytes 12292
  19.3 2.7 copy-start.53
  19.3 2.7 copy-start.49
  19.3 2.7 copy-start.50
  19.3 2.7 copy-start.51
  19.3 2.7 copy-start.48
  19.3 2.7 copy-start.45
  19.3 2.7 copy-start.15
  19.3 2.7 copy-start.31
  21.1 6.6 %copy-start.54 = (s32[2]{0:T(128)S(1)}, s32[2]{0:T(128)}, u32[]{:S(2)}) copy-start(s32[2]{0:T(128)} %param.23) | copy-start | bytes 28
  21.1 6.6 %copy-start.55 = (s32[2]{0:T(128)S(1)}, s32[2]{0:T(128)}, u32[]{:S(2)}) copy-start(s32[2]{0:T(128)} %param.24) | copy-start | bytes 28
  21.1 76.5 %all-gather.3.cloned.1.call-start = ((), (), s32[]{:S(2)}) async-start(), calls=%async_computation.2 | async-start | bytes 5242880 | tf_op jit(solution)/shard_map/all_gather | solution.py:180
  21.9 337.6 %all-reduce.4.cloned.1.call-start = ((), (), s32[]{:S(2)}) async-start(), calls=%async_computation.6 | async-start | bytes 12582912 | tf_op jit(solution)/shard_map/psum | solution.py:269
  22.1 109.9 %copy-start.41 = (f32[4096]{0:T(1024)}, f32[4096]{0:T(1024)S(1)}, u32[]{:S(2)}) copy-start(f32[4096]{0:T(1024)S(1)} %convert_element_type.139) | copy-start | bytes 49156
  22.3 0.6 copy-start.21
  25.6 70.2 %copy-start.29 = (bf16[10,16,64]{2,1,0:T(8,128)(2,1)}, bf16[10,16,64]{2,1,0:T(8,128)(2,1)S(1)}, u32[]{:S(2)}) copy-start(bf16[10,16,64]{2,1,0:T(8,128)(2,1)S(1)} %reshape.242) | copy-start | bytes 61444
  25.7 38.9 %copy-start.20 = (bf16[10,16,64]{2,1,0:T(8,128)(2,1)}, bf16[10,16,64]{2,1,0:T(8,128)(2,1)S(1)}, u32[]{:S(2)}) copy-start(bf16[10,16,64]{2,1,0:T(8,128)(2,1)S(1)} %reshape.241) | copy-start | bytes 61444
  27.7 37.0 %copy-start.2 = (bf16[2,256,1024]{1,2,0:T(8,128)(2,1)}, bf16[2,256,1024]{1,2,0:T(8,128)(2,1)S(1)}, u32[]{:S(2)}) copy-start(bf16[2,256,1024]{1,2,0:T(8,128)(2,1)S(1)} %copy.130) | copy-start | bytes 3145732
  27.8 127.2 %copy-start.46 = (bf16[2,256]{1,0:T(2,128)(2,1)}, bf16[2,256]{1,0:T(2,128)(2,1)S(1)}, u32[]{:S(2)}) copy-start(bf16[2,256]{1,0:T(2,128)(2,1)S(1)} %and_convert_fusion) | copy-start | bytes 3076
  64.6 16.2 %copy-start.12 = (f32[2,16,256,10]{2,3,0,1:T(8,128)S(1)}, f32[2,16,256,10]{2,3,0,1:T(8,128)}, u32[]{:S(2)}) copy-start(f32[2,16,256,10]{2,3,0,1:T(8,128)} %get-tuple-element.138) | copy-start | bytes 983044
  64.6 16.4 %copy-start.8 = (pred[2,256,1024]{2,1,0:T(8,128)(4,1)S(1)}, pred[2,256,1024]{2,1,0:T(8,128)(4,1)}, u32[]{:S(2)}) copy-start(pred[2,256,1024]{2,1,0:T(8,128)(4,1)} %broadcast_and_fusion) | copy-start | bytes 1572868
  80.8 79.6 %copy-start.22 = (f32[2,16,256]{2,1,0:T(8,128)}, f32[2,16,256]{2,1,0:T(8,128)S(1)}, u32[]{:S(2)}) copy-start(f32[2,16,256]{2,1,0:T(8,128)S(1)} %copy_maximum_fusion) | copy-start | bytes 98308
  95.7 64.7 %copy-start.24 = (f32[2,16,256]{2,1,0:T(8,128)}, f32[2,16,256]{2,1,0:T(8,128)S(1)}, u32[]{:S(2)}) copy-start(f32[2,16,256]{2,1,0:T(8,128)S(1)} %copy_add_fusion.1) | copy-start | bytes 98308
  97.6 6.2 %copy-start.9 = (pred[2,256,1024]{2,1,0:T(8,128)(4,1)S(1)}, pred[2,256,1024]{2,1,0:T(8,128)(4,1)}, u32[]{:S(2)}) copy-start(pred[2,256,1024]{2,1,0:T(8,128)(4,1)} %broadcast_and_fusion) | copy-start | bytes 1572868
  103.8 15.7 %copy-start.4 = (bf16[2,256,1024]{2,1,0:T(8,128)(2,1)S(1)}, bf16[2,256,1024]{2,1,0:T(8,128)(2,1)}, u32[]{:S(2)}) copy-start(bf16[2,256,1024]{2,1,0:T(8,128)(2,1)} %param.21) | copy-start | bytes 3145732
  120.9 33.3 %copy-start.6 = (f32[2,256,1024]{2,1,0:T(8,128)}, f32[2,256,1024]{2,1,0:T(8,128)S(1)}, u32[]{:S(2)}) copy-start(f32[2,256,1024]{2,1,0:T(8,128)S(1)} %get-tuple-element.140) | copy-start | bytes 6291460
  121.3 10.7 %copy-start.17 = (bf16[2,256,1024]{2,1,0:T(8,128)(2,1)S(1)}, bf16[2,256,1024]{2,1,0:T(8,128)(2,1)}, u32[]{:S(2)}) copy-start(bf16[2,256,1024]{2,1,0:T(8,128)(2,1)} %param.22) | copy-start | bytes 3145732
  121.3 26.2 %slice-start = ((s8[8388608]{0:T(1024)(128)(4,1)}), s8[4194304]{0:T(1024)(128)(4,1)S(1)}, s32[]{:S(2)}) async-start(s8[8388608]{0:T(1024)(128)(4,1)} %bitcast.128), calls=%async_computation.7 | async-start | bytes 8388608
  132.0 15.5 %slice-start.1 = ((s8[8388608]{0:T(1024)(128)(4,1)}), s8[4194304]{0:T(1024)(128)(4,1)S(1)}, s32[]{:S(2)}) async-start(s8[8388608]{0:T(1024)(128)(4,1)} %bitcast.128), calls=%async_computation.8 | async-start | bytes 8388608
  154.9 1.3 copy-start.10
  154.9 3.6 copy-start.43
  156.2 3.8 copy-start.13
  160.4 27.4 %copy-start.30 = (bf16[10,16,64]{2,1,0:T(8,128)(2,1)S(1)}, bf16[10,16,64]{2,1,0:T(8,128)(2,1)}, u32[]{:S(2)}) copy-start(bf16[10,16,64]{2,1,0:T(8,128)(2,1)} %copy-done.29) | copy-start | bytes 61444
  187.0 1.9 copy-start.3
  188.1 0.6 copy-start.26
  188.9 11.1 %copy-start.32 = (bf16[10,1024]{1,0:T(8,128)(2,1)S(1)}, bf16[10,1024]{1,0:T(8,128)(2,1)}, u32[]{:S(2)}) copy-start(bf16[10,1024]{1,0:T(8,128)(2,1)} %param.37) | copy-start | bytes 61444
  194.2 8.2 %copy-start.28 = (f32[10,512]{1,0:T(8,128)}, f32[10,512]{1,0:T(8,128)S(1)}, u32[]{:S(2)}) copy-start(f32[10,512]{1,0:T(8,128)S(1)} %get-tuple-element.150) | copy-start | bytes 61444
  200.0 2.5 copy-start.23
  200.0 2.5 copy-start.25
  202.4 203.7 %reduce-scatter.5.cloned.1.call-start = ((), (), s32[]{:S(2)}) async-start(), calls=%async_computation.5 | async-start | bytes 5242880 | tf_op jit(solution)/shard_map/reduce_scatter | solution.py:256
  224.7 0.8 copy-start.27
  224.8 228.3 %reduce-scatter.3.cloned.1.call-start = ((), (), s32[]{:S(2)}) async-start(), calls=%async_computation.4 | async-start | bytes 5242880 | tf_op jit(solution)/shard_map/reduce_scatter | solution.py:253
  271.8 0.7 copy-start.52
  286.7 5.5 %copy-start.16 = (bf16[1024,512]{1,0:T(8,128)(2,1)S(1)}, bf16[1024,512]{1,0:T(8,128)(2,1)}, u32[]{:S(2)}) copy-start(bf16[1024,512]{1,0:T(8,128)(2,1)} %param.38) | copy-start | bytes 3145732
  286.7 49.3 %copy-start.7 = (f32[2,256,1024]{2,1,0:T(8,128)S(1)}, f32[2,256,1024]{2,1,0:T(8,128)}, u32[]{:S(2)}) copy-start(f32[2,256,1024]{2,1,0:T(8,128)} %copy-done.6) | copy-start | bytes 6291460
  286.7 49.3 %copy-start.42 = (f32[4096]{0:T(1024)S(1)}, f32[4096]{0:T(1024)}, u32[]{:S(2)}) copy-start(f32[4096]{0:T(1024)} %copy-done.41) | copy-start | bytes 49156
  348.7 104.4 %copy-start.5 = (bf16[2,256,1024]{2,1,0:T(8,128)(2,1)S(1)}, bf16[2,256,1024]{2,1,0:T(8,128)(2,1)}, u32[]{:S(2)}) copy-start(bf16[2,256,1024]{2,1,0:T(8,128)(2,1)} %param.21) | copy-start | bytes 3145732
  348.7 104.4 %copy-start.19 = (bf16[2,256,1024]{2,1,0:T(8,128)(2,1)S(1)}, bf16[2,256,1024]{2,1,0:T(8,128)(2,1)}, u32[]{:S(2)}) copy-start(bf16[2,256,1024]{2,1,0:T(8,128)(2,1)} %copy.150) | copy-start | bytes 3145732
  348.7 104.4 %copy-start.34 = (f32[1024]{0:T(1024)S(1)}, f32[1024]{0:T(1024)}, u32[]{:S(2)}) copy-start(f32[1024]{0:T(1024)} %copy-done.33) | copy-start | bytes 12292
  348.7 104.4 %copy-start.36 = (f32[2,256]{1,0:T(2,128)S(1)}, f32[2,256]{1,0:T(2,128)}, u32[]{:S(2)}) copy-start(f32[2,256]{1,0:T(2,128)} %copy-done.35) | copy-start | bytes 6148
  362.4 97.7 %copy-start.40 = (f32[2,256]{1,0:T(2,128)S(1)}, f32[2,256]{1,0:T(2,128)}, u32[]{:S(2)}) copy-start(f32[2,256]{1,0:T(2,128)} %copy-done.39) | copy-start | bytes 6148
  362.4 97.7 %copy-start.38 = (f32[2,256]{1,0:T(2,128)S(1)}, f32[2,256]{1,0:T(2,128)}, u32[]{:S(2)}) copy-start(f32[2,256]{1,0:T(2,128)} %copy-done.37) | copy-start | bytes 6148
  362.4 98.5 %copy-start.18 = (bf16[2,256,1024]{2,1,0:T(8,128)(2,1)S(1)}, bf16[2,256,1024]{2,1,0:T(8,128)(2,1)}, u32[]{:S(2)}) copy-start(bf16[2,256,1024]{2,1,0:T(8,128)(2,1)} %param.22) | copy-start | bytes 3145732
  362.4 98.5 %copy-start.44 = (f32[2,256]{1,0:T(2,128)S(1)}, f32[2,256]{1,0:T(2,128)}, u32[]{:S(2)}) copy-start(f32[2,256]{1,0:T(2,128)} %copy-done.43) | copy-start | bytes 6148
  362.4 98.5 %copy-start.47 = (bf16[2,256]{1,0:T(2,128)(2,1)S(1)}, bf16[2,256]{1,0:T(2,128)(2,1)}, u32[]{:S(2)}) copy-start(bf16[2,256]{1,0:T(2,128)(2,1)} %copy-done.46) | copy-start | bytes 3076
  460.1 1.6 copy-start.11
  460.9 2.7 copy-start.14
  463.6 3.1 copy-start.1
Sparse Core Ops, SparseCore 0:
  21.2 37.1 all-gather.4
  60.6 34.5 all-gather.2
  202.5 156.9 all-reduce.3
  362.0 44.0 reduce-scatter.4
  408.5 44.4 reduce-scatter.2
where the time goes:
time: 479 us; the launch traced here: 473 us
  matrix products  186 us (39%)
  waiting for transfers between devices  130 us (27%)
  other arithmetic  56.9 us (12%)
  local copies, waits for them, and re-layouts  43.4 us (9%)
  blocking collectives  42.1 us (9%)
  between operations  14.8 us (3%)
    reduce_scatter x1, waiting for transfers between devices, on_device(): lax.psum_scatter(key_terms.astype(jnp.bfloat16), 'seq', scatter_dimension...  46.9 us
    reduce_scatter x1, waiting for transfers between devices, on_device(): lax.psum_scatter(val_terms.astype(jnp.bfloat16), 'seq', scatter_dimension...  43.7 us
    psum x1, blocking collectives, on_device(): lax.psum((grad_embed, grad_midw, grad_midb, grad_kvw, grad_kvb), ('dp', '...  42.1 us
    convert_element_type x1, other arithmetic, query_back(): (token_probs * (token_dprob - delta_rows[..., None])).astype(jnp.bfloat16)  29 us
    all_gather x1, waiting for transfers between devices, on_device(): lax.all_gather(keys_loc, 'seq', axis=1, tiled=True)  28.2 us
    dot_general x1, matrix products, query_back(): jnp.einsum('gqhe,gkhe->ghqk', grad_heads, vals_all, preferred_element_typ...  26.6 us
    dot_general x1, matrix products, head_scores(): jnp.einsum('gqhe,gkhe->ghqk', queries, keys_all, preferred_element_type=j...  16.1 us
    dot_general x1, matrix products, query_back(): jnp.einsum('ghqk,gqhe->gkhe', token_probs.astype(jnp.bfloat16), grad_head...  15.9 us
  transfers between devices with their start and end apart: 5, of which 4 were waited for; matrix products, arithmetic and copies ran while one was open for 32% of the time, Pallas kernels for 0%

commit v1 on v0

v1 whole, which is shorter than its diff:
```python
import jax
import jax.numpy as jnp
from jax import lax
from jax.experimental import pallas as pl
from jax.experimental.pallas import tpu as pltpu
from jax.sharding import PartitionSpec as P

D = 1024
HD = 64
FF = 4096
PRE = 10
PP = 16
SEG = 256
OWN = 512
NH = 8
NB = 4
EPS = 1e-05
NEG = -1e30
HIGH = lax.Precision.HIGHEST
MESH = pl.DeviceIdType.MESH
f32 = jnp.float32
bf16 = jnp.bfloat16


def mm(a, b, ca=1, cb=0):
    return lax.dot_general(a, b, (((ca,), (cb,)), ((), ())), preferred_element_type=f32)


def centre(v):
    mean = jnp.mean(v, axis=-1, keepdims=True)
    cen = v - mean
    var = jnp.mean(cen * cen, axis=-1, keepdims=True)
    return cen, lax.rsqrt(var + EPS)


def norm_back(v, incoming):
    cen, r = centre(v)
    xhat = cen * r
    m1 = jnp.mean(incoming, axis=-1, keepdims=True)
    m2 = jnp.mean(incoming * xhat, axis=-1, keepdims=True)
    return r * (incoming - m1 - xhat * m2)


def aligned(i, n):
    return pl.multiple_of(i, n)


def split3(v):
    hi = v.astype(bf16)
    rest = v - hi.astype(f32)
    mid = rest.astype(bf16)
    lo = (rest - mid.astype(f32)).astype(bf16)
    return hi, mid, lo


def kernel(
    tok_h, cot_h, src, tgt,
    ag1, ash1, qb1, ob1, mg1, msh1, fb1, pb1, mb1, kvb1,
    wqkv_h, wout_h, wfc_h, wproj_h, emb, midw_h, kvw_h,
    hid_h, gtok_h, gpre,
    wqkv, wout, wfc, wproj,
    tok2, cot2, xn, qm, kx, kT, vx, vT, es, ep, dsp, ot, oTo, oTf,
    mid, yacc, dxacc, dqT, kb, dbias,
    pkT, pvbd, pvT, linv, deltap,
    ag, ash, qb, ob, mg, msh, fb, pb, kvb,
    wsem, lsem, far_s, far_r, xn_s, xn_r, o_s, o_r, d_s, d_r, g_s, g_r, out_s, out_r, loc_out,
):
    s = lax.axis_index("seq")
    y = lax.div(s, 2)
    c = lax.rem(s, 2)
    sib = 2 * y + (1 - c)
    far = 2 * (1 - y) + c
    bl = 2 * y + c
    br = 2 * (1 - y) + c
    cw = aligned(c * OWN, OWN)
    ow = aligned((1 - c) * OWN, OWN)

    def load(i, src_ref, dst_ref):
        cp = pltpu.make_async_copy(src_ref, dst_ref, wsem.at[i])
        cp.start()
        return cp

    ld_tok = load(0, tok_h.at[y], tok2.at[pl.ds(0, SEG)])
    ld_mid0 = load(1, midw_h.at[pl.ds(0, 512)], vT.at[:, pl.ds(0, 512)])
    ld_mid1 = load(2, midw_h.at[pl.ds(512, 512)], vT.at[:, pl.ds(512, 512)])
    ld_kvk = load(3, kvw_h.at[:, pl.ds(cw, OWN)], kT.at[:, pl.ds(0, OWN)])
    ld_kvv = load(4, kvw_h.at[:, pl.ds(aligned(D + c * OWN, OWN), OWN)], kT.at[:, pl.ds(OWN, OWN)])
    ld_qkv = load(5, wqkv_h, wqkv)
    ld_cot = load(6, cot_h.at[y], cot2.at[pl.ds(0, SEG)])
    ld_out = load(7, wout_h, wout)
    ld_fc = load(8, wfc_h, wfc)
    ld_proj = load(9, wproj_h, wproj)

    barrier = pltpu.get_barrier_semaphore()
    for peer in (sib, far):
        pl.semaphore_signal(barrier, inc=1, device_id={"seq": peer}, device_id_type=MESH)
    pl.semaphore_wait(barrier, 2)

    def remote(src_ref, dst_ref, ss, rs, peer):
        return pltpu.make_async_remote_copy(
            src_ref=src_ref, dst_ref=dst_ref, send_sem=ss, recv_sem=rs,
            device_id={"seq": peer}, device_id_type=MESH,
        )

    CH = 64
    NCH = SEG // CH
    tok_cp = [
        remote(
            tok_h.at[1 - y, pl.ds(j * CH, CH)], tok2.at[pl.ds(SEG + j * CH, CH)],
            far_s.at[j], far_r.at[j], far,
        )
        for j in range(NCH)
    ]
    for cp in tok_cp:
        cp.start()
    cot_cp = remote(cot_h.at[1 - y], cot2.at[pl.ds(SEG, SEG)], far_s.at[NCH], far_r.at[NCH], far)

    for dst, vec in ((ag, ag1), (ash, ash1), (qb, qb1), (ob, ob1), (mg, mg1), (msh, msh1), (fb, fb1), (pb, pb1), (kvb, kvb1)):
        n = vec.shape[0]
        for i in range(0, n, 1024):
            dst[:, i : i + 1024] = vec[pl.ds(i, 1024)].astype(f32).reshape(1, 1024)
    total = src[y] + tgt[y]
    start = src[y]
    rowp = lax.broadcasted_iota(jnp.int32, (PP, 128), 0)
    kb[0:PP, :] = jnp.where(rowp < PRE, 0.0, NEG)
    for b in range(NB):
        pos = lax.broadcasted_iota(jnp.int32, (SEG, 128), 0) + b * SEG
        kb[PP + b * SEG : PP + (b + 1) * SEG, :] = jnp.where(pos < total, 0.0, NEG)

    def norm_rows(row0, n, dst0):
        cen, r = centre(tok2[row0 : row0 + n, :].astype(f32))
        xn[pl.ds(aligned(dst0, n), n), :] = (cen * r * ag[...] + ash[...]).astype(bf16)

    ld_tok.wait()
    norm_rows(0, SEG, bl * SEG)
    xl = xn.at[pl.ds(aligned(bl * SEG, SEG), SEG)]
    xl_cp = remote(xl, xl, xn_s.at[NCH], xn_r.at[NCH], sib)
    xl_cp.start()

    ld_mid0.wait()
    ld_mid1.wait()
    embp = jnp.concatenate([emb[...], jnp.zeros((PP - PRE, D), bf16)], axis=0)
    pre = mm(embp[:, 0:512], vT[:, 0:512]) + mm(embp[:, 512:1024], vT[:, 512:1024])
    pre = pre + mb1[...].astype(f32).reshape(1, 512)
    hidden = jnp.tanh(pre)
    ld_kvk.wait()
    ld_kvv.wait()
    h3 = jnp.concatenate(split3(hidden), axis=0)
    pk3 = mm(h3, kT[:, 0:OWN])
    pv3 = mm(h3, kT[:, OWN : 2 * OWN])
    pk = pk3[0:PP] + pk3[PP : 2 * PP] + pk3[2 * PP :] + kvb[:, pl.ds(cw, OWN)]
    pv = pv3[0:PP] + pv3[PP : 2 * PP] + pv3[2 * PP :] + kvb[:, pl.ds(aligned(D + c * OWN, OWN), OWN)]
    for hp in range(4):
        kx[hp, 0:PP, :] = pk[:, hp * 128 : (hp + 1) * 128].astype(bf16)
    hr = lax.broadcasted_iota(jnp.int32, (NH * PP, OWN), 0) // PP
    hc = lax.broadcasted_iota(jnp.int32, (NH * PP, OWN), 1) // HD
    pk8 = jnp.where(hr == hc, jnp.concatenate([pk] * NH, axis=0), 0.0)
    pv8 = jnp.where(hr == hc, jnp.concatenate([pv] * NH, axis=0), 0.0)
    pvbd[...] = pv8.astype(bf16)
    pkT[...] = pk8.T.astype(bf16)
    pvT[...] = pv8.T.astype(bf16)

    lane = lax.broadcasted_iota(jnp.int32, (1, 128), 1)
    lo_half = jnp.where(lane < HD, 1.0, 0.0).astype(bf16)
    hi_half = jnp.where(lane < HD, 0.0, 1.0).astype(bf16)

    def spread(dst, rows, val):
        for hp in range(4):
            pair = val[:, hp * 128 : (hp + 1) * 128]
            dst[rows, 2 * hp * 128 : (2 * hp + 1) * 128] = pair * lo_half
            dst[rows, (2 * hp + 1) * 128 : (2 * hp + 2) * 128] = pair * hi_half

    def project(b):
        rows = pl.ds(aligned(b * SEG, SEG), SEG)
        krows = pl.ds(aligned(PP + b * SEG, PP), SEG)
        x = xn[rows, :]
        q = (mm(x, wqkv[:, pl.ds(cw, OWN)]) + qb[:, pl.ds(cw, OWN)]).astype(bf16) * jnp.asarray(HD ** (-0.5), bf16)
        spread(qm, rows, q)
        kw = pl.ds(aligned(D + c * OWN, OWN), OWN)
        k = (mm(x, wqkv[:, kw]) + qb[:, kw]).astype(bf16)
        kT[:, rows] = k.T
        vw = pl.ds(aligned(2 * D + c * OWN, OWN), OWN)
        v = (mm(x, wqkv[:, vw]) + qb[:, vw]).astype(bf16)
        vT[:, rows] = v.T
        for hp in range(4):
            kx[hp, krows, :] = k[:, hp * 128 : (hp + 1) * 128]
            vx[hp, rows, :] = v[:, hp * 128 : (hp + 1) * 128]

    ld_qkv.wait()
    project(bl)
    xl_cp.wait()
    project(lax.bitwise_xor(bl, 1))

    fw = []
    for j in range(NCH):
        tok_cp[j].wait_recv()
        norm_rows(SEG + j * CH, CH, br * SEG + j * CH)
        xr = xn.at[pl.ds(aligned(br * SEG + j * CH, CH), CH)]
        cp = remote(xr, xr, xn_s.at[j], xn_r.at[j], sib)
        cp.start()
        fw.append(cp)
    for cp in tok_cp:
        cp.wait_send()
    cot_cp.start()
    project(br)
    for cp in fw:
        cp.wait()
    project(lax.bitwise_xor(br, 1))

    def slot_of(b):
        return lax.bitwise_xor(b // 2 if isinstance(b, int) else lax.div(b, 2), y)

    def rep(vals, n):
        return jnp.concatenate([jnp.broadcast_to(vals[h : h + 1], (n, vals.shape[1])) for h in range(NH)], axis=0)

    def twice(v):
        return jnp.concatenate([v, v], axis=1)

    tri = lax.broadcasted_iota(jnp.int32, (SEG, SEG), 0) <= lax.broadcasted_iota(jnp.int32, (SEG, SEG), 1)

    def o_copy(b):
        return remote(
            oTo.at[b], oTf.at[slot_of(b), pl.ds(cw, OWN)], o_s.at[slot_of(b)], o_r.at[slot_of(b)], sib
        )

    for b in (3, 2, 1, 0):
        cols = slice(b * SEG, (b + 1) * SEG)
        low = PP + b * SEG
        off = SEG * (b * (b + 1) // 2)
        dbias[...] = jnp.where(tri, twice(kb[low : low + SEG, :]), NEG)

        def heads(hp, carry, b=b, cols=cols, low=low, off=off):
            for u in range(2):
                h = 2 * hp + u
                qh = qm[cols, pl.ds(aligned(h * 128, 128), 128)]
                s0 = mm(kx[hp, 0:low, :], qh, 1, 1) + twice(kb[0:low, :])
                s1 = mm(kx[hp, low : low + SEG, :], qh, 1, 1) + dbias[...]
                m = jnp.maximum(jnp.max(s0, axis=0, keepdims=True), jnp.max(s1, axis=0, keepdims=True))
                e0 = jnp.exp(s0 - m)
                e1 = jnp.exp(s1 - m)
                den = jnp.sum(e0, axis=0, keepdims=True) + jnp.sum(e1, axis=0, keepdims=True)
                linv[pl.ds(h, 1), cols] = 1.0 / den
                p0 = e0.astype(bf16)
                p1 = e1.astype(bf16)
                ep[pl.ds(aligned(h * PP, PP), PP), cols] = p0[0:PP]
                hrows = pl.ds(aligned(h * HD, HD), HD)
                if b:
                    es[h, off : off + b * SEG, :] = p0[PP:]
                es[h, off + b * SEG : off + (b + 1) * SEG, :] = p1
                ot[hrows, :] = mm(vT[hrows, 0 : (b + 1) * SEG], es[h, off : off + (b + 1) * SEG, :])
            return carry

        lax.fori_loop(0, 4, heads, 0)
        o = (ot[...] + mm(pvT[...], ep[:, cols])) * rep(linv[:, cols], HD)
        oTo[b] = o.astype(bf16)

        @pl.when(c == b % 2)
        def _(b=b):
            oTf[slot_of(b), pl.ds(cw, OWN), :] = oTo[b]

        @pl.when(c != b % 2)
        def _(b=b):
            o_copy(b).start()

    def half_get(ref, sl):
        return jnp.concatenate([ref[sl * SEG : (sl + 1) * SEG, :], ref[OWN + sl * SEG : OWN + (sl + 1) * SEG, :]], axis=1)

    def half_put(ref, sl, val):
        ref[sl * SEG : (sl + 1) * SEG, :] = val[:, 0:OWN]
        ref[OWN + sl * SEG : OWN + (sl + 1) * SEG, :] = val[:, OWN:]

    ld_out.wait()
    ld_cot.wait()
    cot_cp.wait_recv()
    for sl in (0, 1):
        pltpu.make_async_copy(oTf.at[sl, pl.ds(ow, OWN)], oTf.at[sl, pl.ds(ow, OWN)], o_r.at[sl]).wait()
        blk = bl if sl == 0 else br
        m = mm(oTf[sl], wout[...], 0, 0) + ob[...] + tok2[sl * SEG : (sl + 1) * SEG, :].astype(f32)
        half_put(mid, sl, m)
        cen, r = centre(m)
        xn[sl * SEG : (sl + 1) * SEG, :] = (cen * r * mg[...] + msh[...]).astype(bf16)
        pos = lax.broadcasted_iota(jnp.int32, (SEG, 1), 0) + blk * SEG
        seen = jnp.where((pos >= start) & (pos < total), 1.0, 0.0)
        cot2[sl * SEG : (sl + 1) * SEG, :] = (cot2[sl * SEG : (sl + 1) * SEG, :].astype(f32) * seen).astype(bf16)
    for sl in (0, 1):
        pltpu.make_async_copy(oTo.at[sl], oTo.at[sl], o_s.at[sl]).wait()

    ld_fc.wait()
    ld_proj.wait()
    yacc[...] = jnp.zeros_like(yacc)
    dxacc[...] = jnp.zeros_like(dxacc)
    FC = 512

    def feed(i, carry):
        fs = pl.ds(aligned(i * FC, FC), FC)
        u = mm(xn[0:OWN, :], wfc[:, fs]) + fb[:, fs]
        da = mm(cot2[...], wproj[fs, :], 1, 1)
        u2 = u * u
        th = jnp.tanh(u * (0.7978845608028654 + 0.035677408136300125 * u2))
        hh = 0.5 * th + 0.5
        act = u * hh
        slope = hh + act * (1.0 - hh) * (1.5957691216057308 + 0.21406444881780075 * u2)
        ab = act.astype(bf16)
        db = (slope * da).astype(bf16)
        for n in range(2):
            rows = slice(n * OWN, (n + 1) * OWN)
            yacc[rows, :] += mm(ab, wproj[fs, rows])
            dxacc[rows, :] += mm(db, wfc[rows, fs], 1, 1)
        return carry

    lax.fori_loop(0, FF // FC, feed, 0)

    for sl in (1, 0):
        out = half_get(mid, sl) + half_get(yacc, sl) + pb[...]
        xn[sl * SEG : (sl + 1) * SEG, :] = out.astype(bf16)
    hid_cp = remote(xn.at[pl.ds(SEG, SEG)], hid_h.at[y], out_s.at[0], out_r.at[0], far)
    hid_cp.start()
    hid_lo = pltpu.make_async_copy(xn.at[pl.ds(0, SEG)], hid_h.at[y], loc_out.at[0])
    hid_lo.start()

    def do_copy(sl):
        blk = bl if sl == 0 else br
        dst = xn.at[pl.ds(OWN, OWN), pl.ds(aligned(blk * SEG, SEG), SEG)]
        return remote(oTf.at[sl, pl.ds(0, OWN)], dst, d_s.at[sl], d_r.at[sl], sib)

    for sl in (0, 1):
        blk = bl if sl == 0 else br
        rows = slice(sl * SEG, (sl + 1) * SEG)
        gm = cot2[rows, :].astype(f32) + norm_back(half_get(mid, sl), half_get(dxacc, sl) * mg[...])
        half_put(dxacc, sl, gm)
        gmb = gm.astype(bf16)
        oTf[sl, 0:OWN, :] = mm(wout[pl.ds(ow, OWN), :], gmb, 1, 1).astype(bf16)
        do_copy(sl).start()
        xn[OWN:D, pl.ds(aligned(blk * SEG, SEG), SEG)] = mm(wout[pl.ds(cw, OWN), :], gmb, 1, 1).astype(bf16)

    dk = yacc
    dv = mid
    dk[...] = jnp.zeros_like(dk)
    dv[...] = jnp.zeros_like(dv)
    for cp in (do_copy(0), do_copy(1)):
        cp.wait()
    for b in range(NB):
        cols = slice(b * SEG, (b + 1) * SEG)
        li = linv[:, cols]
        dof = xn[OWN:D, cols].astype(f32)
        prod = dof * oTo[b].astype(f32)
        dl = jnp.concatenate(
            [jnp.sum(prod[h * HD : (h + 1) * HD], axis=0, keepdims=True) for h in range(NH)], axis=0
        ) * li
        deltap[:, cols] = dl
        dos = (dof * rep(li, HD)).astype(bf16)
        spread(wproj, cols, dos.T)
        dpp = mm(pvbd[...], dos)
        dsb = (ep[:, cols].astype(f32) * (dpp - rep(dl, PP))).astype(bf16)
        dsp[:, cols] = dsb
        dqT[:, cols] = mm(pkT[...], dsb)

    def prefix_grad(left, right, at):
        for n in range(2):
            t = mm(left, right[0:1024, n * 512 : (n + 1) * 512])
            for p in range(2):
                h = 4 * n + 2 * p
                v = t[h * PP : (h + 1) * PP, 2 * p * 128 : (2 * p + 1) * 128]
                v = v + t[(h + 1) * PP : (h + 2) * PP, (2 * p + 1) * 128 : (2 * p + 2) * 128]
                gpre[:, at + h * HD : at + h * HD + 128] = v

    prefix_grad(dsp[...], qm, 0)
    prefix_grad(ep[...], wproj, OWN)

    def at_tile(i, j):
        qi = jnp.where(y == 1, j, 3 - i)
        ki = jnp.where(y == 1, i, 3 - j)
        return qi, ki

    def tile(i, j):
        qi, ki = at_tile(i, j)
        qr = pl.ds(aligned(qi * SEG, SEG), SEG)
        kr = pl.ds(aligned(ki * SEG, SEG), SEG)
        off = pl.ds(aligned((lax.div(qi * (qi + 1), 2) + ki) * SEG, SEG), SEG)
        for hp in range(4):
            hl = slice(hp * 128, (hp + 1) * 128)
            gk = dk[kr, hl]
            gv = dv[kr, hl]
            for u in range(2):
                h = 2 * hp + u
                hw = slice(h * 128, (h + 1) * 128)
                hrows = slice(h * HD, (h + 1) * HD)
                doh = wproj[qr, hw]
                e = es[h, off, :]
                dp = mm(vx[hp, kr, :], doh, 1, 1)
                ds = (e.astype(f32) * (dp - deltap[h : h + 1, qr])).astype(bf16)
                gv = gv + mm(e, doh)
                gk = gk + mm(ds, qm[qr, hw])
                dqT[hrows, qr] += mm(kT[hrows, kr], ds)
            dk[kr, hl] = gk
            dv[kr, hl] = gv

    def block_at(i):
        return jnp.where(y == 1, i, 3 - i)

    def d_copy(b, i):
        sl = slot_of(b)
        return remote(
            wfc.at[pl.ds(aligned(sl * SEG, SEG), SEG), pl.ds(2048, 1536)],
            wfc.at[pl.ds(aligned((2 * sl + c) * SEG, SEG), SEG), pl.ds(0, 1536)],
            g_s.at[i // 2], g_r.at[i // 2], sib,
        )

    def done_block(i):
        b = block_at(i)
        br_ = pl.ds(aligned(b * SEG, SEG), SEG)
        sl = slot_of(b)
        mine = lax.rem(b, 2) == c
        parts = (
            (dqT[:, br_] * HD ** (-0.5)).astype(bf16).T,
            dk[br_, :].astype(bf16),
            dv[br_, :].astype(bf16),
        )
        row = aligned(jnp.where(mine, 2 * sl + c, sl) * SEG, SEG)
        for p in range(3):
            col = aligned(jnp.where(mine, 0, 2048) + p * 512, 512)
            wfc[pl.ds(row, SEG), pl.ds(col, 512)] = parts[p]

        @pl.when(jnp.logical_not(mine))
        def _():
            d_copy(b, i).start()

    def finish(i):
        b = block_at(i)
        sl = slot_of(b)

        @pl.when(lax.rem(b, 2) == c)
        def _():
            d_copy(b, i).wait_recv()
            acc = None
            for p in range(3):
                for hf in range(2):
                    a = wfc[pl.ds(aligned((2 * sl + hf) * SEG, SEG), SEG), p * 512 : (p + 1) * 512]
                    t = mm(a, wqkv[:, p * D + hf * OWN : p * D + (hf + 1) * OWN], 1, 1)
                    acc = t if acc is None else acc + t
            rows = pl.ds(aligned(sl * SEG, SEG), SEG)
            rows2 = pl.ds(aligned(OWN + sl * SEG, SEG), SEG)
            gm = jnp.concatenate([dxacc[rows, :], dxacc[rows2, :]], axis=1)
            res = gm + norm_back(tok2[rows, :].astype(f32), acc * ag[...])
            xn[rows, :] = res.astype(bf16)
            if i < 2:
                gt_cp().start()
            else:
                gt_lo().start()

    def gt_cp():
        return remote(xn.at[pl.ds(SEG, SEG)], gtok_h.at[y], out_s.at[1], out_r.at[1], far)

    def gt_lo():
        return pltpu.make_async_copy(xn.at[pl.ds(0, SEG)], gtok_h.at[y], loc_out.at[1])

    hid_cp.wait_send()
    hid_lo.wait()
    cot_cp.wait_send()
    for i in range(4):
        lax.fori_loop(i, 4, lambda j, carry, i=i: (tile(i, j), carry)[1], 0)
        done_block(i)
        if i:
            finish(i - 1)
    finish(3)

    for i in range(2):
        pltpu.make_async_copy(
            wfc.at[pl.ds(0, SEG), pl.ds(2048, 1536)], wfc.at[pl.ds(0, SEG), pl.ds(2048, 1536)], g_s.at[i]
        ).wait()
    gt_lo().wait()
    gt_cp().wait()
    hid_cp.wait_recv()


def layer(args):
    vm = pl.BlockSpec(memory_space=pltpu.VMEM)
    hb = pl.BlockSpec(memory_space=pl.ANY)
    sm = pl.BlockSpec(memory_space=pltpu.SMEM)
    (tokens, cotangent, src_len, tgt_len, attn_gain, attn_shift, qkv_weight, qkv_bias, out_weight, out_bias,
     mlp_gain, mlp_shift, fc_weight, fc_bias, proj_weight, proj_bias, embed_rows, mid_weight, mid_bias,
     kv_weight, kv_bias) = args
    V = pltpu.VMEM
    dma = pltpu.SemaphoreType.DMA
    return pl.pallas_call(
        kernel,
        out_shape=(
            jax.ShapeDtypeStruct(tokens.shape, bf16),
            jax.ShapeDtypeStruct(tokens.shape, bf16),
            jax.ShapeDtypeStruct((PP, D), f32),
        ),
        in_specs=[hb, hb, sm, sm] + [vm] * 10 + [hb] * 4 + [vm, hb, hb],
        out_specs=(hb, hb, vm),
        scratch_shapes=[
            V((D, 3 * D), bf16), V((D, D), bf16), V((D, FF), bf16), V((FF, D), bf16),
            V((OWN, D), bf16), V((OWN, D), bf16), V((D, D), bf16), V((D, D), bf16),
            V((4, PP + D, 128), bf16), V((OWN, D), bf16), V((4, D, 128), bf16), V((OWN, D), bf16),
            V((NH, 10 * SEG, SEG), bf16), V((NH * PP, D), bf16), V((NH * PP, D), bf16),
            V((OWN, SEG), f32), V((NB, OWN, SEG), bf16), V((2, D, SEG), bf16),
            V((D, OWN), f32), V((D, OWN), f32), V((D, OWN), f32),
            V((OWN, D), f32), V((PP + D, 128), f32), V((SEG, SEG), f32),
            V((OWN, NH * PP), bf16), V((NH * PP, OWN), bf16), V((OWN, NH * PP), bf16),
            V((NH, D), f32), V((NH, D), f32),
            V((1, D), f32), V((1, D), f32), V((1, 3 * D), f32), V((1, D), f32), V((1, D), f32), V((1, D), f32),
            V((1, FF), f32), V((1, D), f32), V((1, 2 * D), f32),
            dma((10,)), dma((1,)), dma((5,)), dma((5,)), dma((5,)), dma((5,)), dma((2,)), dma((2,)),
            dma((2,)), dma((2,)), dma((2,)), dma((2,)), dma((2,)), dma((2,)), dma((2,)),
        ],
        compiler_params=pltpu.CompilerParams(
            collective_id=0, has_side_effects=True, vmem_limit_bytes=64 << 20
        ),
    )(tokens, cotangent, src_len, tgt_len, attn_gain, attn_shift, qkv_bias, out_bias, mlp_gain, mlp_shift, fc_bias,
      proj_bias, mid_bias, kv_bias, qkv_weight, out_weight, fc_weight, proj_weight, embed_rows, mid_weight, kv_weight)


def reparam_back(grad_prefix, embed_f, midw_f, kvw_f, prefix_hidden):
    grad_kvb = jnp.sum(grad_prefix, axis=0)
    grad_kvw = jnp.dot(prefix_hidden.T, grad_prefix, precision=HIGH)
    grad_pre = jnp.dot(grad_prefix, kvw_f.T, precision=HIGH) * (1.0 - prefix_hidden * prefix_hidden)
    grad_midb = jnp.sum(grad_pre, axis=0)
    grad_midw = jnp.dot(embed_f.T, grad_pre, precision=HIGH)
    grad_embed = jnp.dot(grad_pre, midw_f.T, precision=HIGH)
    return (grad_embed, grad_midw, grad_midb, grad_kvw, grad_kvb)


def on_device(*args):
    embed_rows, mid_weight, mid_bias, kv_weight, kv_bias = args[16:]
    hidden_out, grad_tokens, own = layer(args)
    own = own[:PRE]
    half = lax.rem(lax.axis_index("seq"), 2)
    parts = jnp.where(jnp.arange(2)[None, None, :, None] == half, own.reshape(PRE, 2, 1, OWN), 0.0)
    grad_prefix = lax.psum(parts.reshape(PRE, 2 * D), ("dp", "seq"))
    embed_f = embed_rows.astype(f32)
    midw_f = mid_weight.astype(f32)
    kvw_f = kv_weight.astype(f32)
    prefix_hidden = jnp.tanh(jnp.dot(embed_f, midw_f, precision=HIGH) + mid_bias.astype(f32))
    return (hidden_out, grad_tokens) + reparam_back(grad_prefix, embed_f, midw_f, kvw_f, prefix_hidden)


def solution(mesh):
    split = P("dp", "seq", None)
    return jax.shard_map(
        on_device,
        mesh=mesh,
        in_specs=(split, split, P("dp"), P("dp")) + (P(),) * 17,
        out_specs=(split, split, P(), P(), P(), P(), P()),
        check_vma=False,
    )
```

time: 479 us -> 270 us (0.56)
  matrix products: 186 us -> 13.1 us
  Pallas kernels: 0 us -> 109 us
  other arithmetic: 56.9 us -> 1.98 us
  blocking collectives: 42.1 us -> 0 us
  local copies, waits for them, and re-layouts: 43.4 us -> 4.85 us
  waiting for transfers between devices: 130 us -> 123 us
    dot_general x22 -> x1, matrix products: 172 us -> 1.51 us  [on_device(): jnp.dot(embed_f, midw_f, precision=HIGH) + mid_bias.astype(f32)]
    psum x1, waiting for transfers between devices: 10.8 us -> 123 us  [on_device(): grad_prefix = lax.psum(parts.reshape(PRE, 2 * D), ('dp', 'seq'))]
    pallas_call x0 -> x1, Pallas kernels: none -> 109 us  [layer(): pl.pallas_call(kernel, out_shape=(jax.ShapeDtypeStruct(tokens.shape, bf16...]
    reduce_scatter x2 -> x0, waiting for transfers between devices: 90.7 us -> none  [the longest x1 46.9 us: on_device(): lax.psum_scatter(key_terms.astype(jnp.bfloat16), 'seq', scatter_dimension...]
    psum x1 -> x0, blocking collectives: 42.1 us -> none  [on_device(): lax.psum((grad_embed, grad_midw, grad_midb, grad_kvw, grad_kvb), ('dp', '...]
    convert_element_type x14 -> x1, other arithmetic: 33.9 us -> 0.68 us  [on_device(): mid_bias.astype(f32)]
    all_gather x2 -> x0, waiting for transfers between devices: 28.2 us -> none  [the longest x1 28.2 us: on_device(): lax.all_gather(keys_loc, 'seq', axis=1, tiled=True)]
    reduce_sum x7 -> x0, other arithmetic: 19.8 us -> none  [the longest x2 14.8 us: forward_group(): denoms = jnp.sum(prefix_exp, axis=-1) + jnp.sum(token_exp, axis=-1)]
  transfers between devices with their start and end apart: 5 -> 1, of which waited for: 4 -> 1; matrix products, arithmetic and copies ran while one was open for 32% -> 1% of each run, Pallas kernels for 0% -> 0%
where the time goes in v1:
time: 270 us; the launch traced here: 266 us
  waiting for transfers between devices  123 us (46%)
  Pallas kernels  109 us (40%)
  between operations  14.3 us (5%)
  matrix products  13.1 us (5%)
  local copies, waits for them, and re-layouts  4.85 us (2%)
    psum x1, waiting for transfers between devices, on_device(): grad_prefix = lax.psum(parts.reshape(PRE, 2 * D), ('dp', 'seq'))  123 us
    pallas_call x1, Pallas kernels, layer(): pl.pallas_call(kernel, out_shape=(jax.ShapeDtypeStruct(tokens.shape, bf16...  109 us
  transfers between devices with their start and end apart: 1, of which 1 were waited for; matrix products, arithmetic and copies ran while one was open for 1% of the time, Pallas kernels for 0%

profile of v1, /device:TPU:0, one launch (start us, length us, event | category | flops | bytes accessed | tf_op | source)
XLA Modules:
  0.0 266.3 jit_solution(282586996591686753)
XLA Ops:
  7.2 0.0 all-reduce.2.cloned.1.call-start
  7.2 109.4 %shard_map.252 = (bf16[2,256,1024]{2,1,0:T(8,128)(2,1)}, bf16[2,256,1024]{2,1,0:T(8,128)(2,1)}, f32[16,1024]{1,0:T(8,128)}) custom-call(bf16[2,256,1024]{2,1,0:T(8,128)(2,1)} %tok_h.1, bf16[2,256,1024]{2,1,0:T(8,128)(2,1)} %cot_h.1, s32[2]{0:T(128)} %src.1, s32[2]{0:T(128)} %tgt.1, bf16[1024]{0:T(1024)(128)(2,1)} %ag1.1, bf16[1024]{0:T(1024)(128)(2,1)} %ash1.1, ...), custom_call_target="tpu_custom_call" | custom-call | tf_op jit(solution)/shard_map/pallas_call | solution.py:485
  116.6 0.9 broadcast_in_dim.33
  117.5 0.0 copy-start
  117.5 0.1 broadcast_in_dim.35
  117.6 0.1 broadcast_in_dim.30
  117.7 0.7 broadcast_select_fusion
  118.4 0.0 all-reduce.2.cloned.1.call-update
  118.4 0.7 convert_element_type.2
  119.1 0.0 copy-start.4
  119.1 1.5 fusion
  120.6 122.7 %all-reduce.2.cloned.1.call-done = f32[10,2048]{1,0:T(8,128)} async-done(((f32[10,2048]{1,0:T(8,128)}), f32[10,2048]{1,0:T(8,128)}) %all-reduce.2.cloned.1.call-update) | async-done | bytes 81936 | tf_op jit(solution)/shard_map/psum | solution.py:532
  243.3 4.0 %fusion.1 = (f32[512]{0:T(512)}, f32[10,512]{1,0:T(8,128)S(1)}) fusion(f32[10,512]{1,0:T(8,128)S(1)} %fusion, f32[10,2048]{1,0:T(8,128)} %all-reduce.2.cloned.1.call-done, bf16[512,2048]{1,0:T(8,128)(2,1)} %kvw_h.1), kind=kOutput, calls=%fused_computation.6 | convolution fusion | flops 125849088 | bytes 2222080 | tf_op jit(solution)/shard_map/dot_general | solution.py:519
  247.3 0.0 copy-done
  247.3 1.6 fusion.2
  248.8 0.0 copy-done.4
  248.8 1.0 convolution_bitcast_fusion
  249.9 0.0 copy-start.1
  249.9 1.8 copy.29
  251.7 0.0 copy-done.1
  251.7 0.0 copy-start.3
  251.7 5.0 %fusion.3 = f32[512,2048]{1,0:T(8,128)} fusion(f32[10,512]{1,0:T(8,128)S(1)} %fusion, f32[10,2048]{1,0:T(8,128)S(1)} %copy-done.1), kind=kOutput, calls=%fused_computation.8 | convolution fusion | flops 125829120 | bytes 4296704 | tf_op jit(solution)/shard_map/dot_general | solution.py:518
  256.7 0.0 copy-start.2
  256.7 0.6 reduce_sum.19
  257.4 0.0 copy-done.3
  257.4 1.0 copy.33
  258.3 0.0 copy-done.2
  258.3 1.0 copy.34
  (3 shorter events, 0.1 us)
Async XLA Ops:
  7.2 236.1 %all-reduce.2.cloned.1.call-start = ((), (), s32[]{:S(2)}) async-start(), calls=%async_computation | async-start | bytes 262144 | tf_op jit(solution)/shard_map/psum | solution.py:532
  117.5 129.8 %copy-start = (bf16[1024,512]{1,0:T(8,128)(2,1)S(1)}, bf16[1024,512]{1,0:T(8,128)(2,1)}, u32[]{:S(2)}) copy-start(bf16[1024,512]{1,0:T(8,128)(2,1)} %midw_h.1) | copy-start | bytes 3145732
  119.1 129.8 %copy-start.4 = (bf16[10,1024]{1,0:T(8,128)(2,1)S(1)}, bf16[10,1024]{1,0:T(8,128)(2,1)}, u32[]{:S(2)}) copy-start(bf16[10,1024]{1,0:T(8,128)(2,1)} %emb.1) | copy-start | bytes 61444
  249.9 1.8 copy-start.1
  251.7 5.6 %copy-start.3 = (bf16[2,256,1024]{2,1,0:T(8,128)(2,1)S(1)}, bf16[2,256,1024]{2,1,0:T(8,128)(2,1)}, u32[]{:S(2)}) copy-start(bf16[2,256,1024]{2,1,0:T(8,128)(2,1)} %get-tuple-element.36) | copy-start | bytes 3145732
  256.7 1.6 copy-start.2
Sparse Core Ops, SparseCore 0:
  118.5 124.7 all-reduce.1

commit v2 on v1

--- a/solution.py
+++ b/solution.py
@@ -1,3 +1,5 @@
+import functools
+
 import jax
 import jax.numpy as jnp
 from jax import lax
@@ -14,9 +16,9 @@
 OWN = 512
 NH = 8
 NB = 4
+NRED = 8
 EPS = 1e-05
 NEG = -1e30
-HIGH = lax.Precision.HIGHEST
 MESH = pl.DeviceIdType.MESH
 f32 = jnp.float32
 bf16 = jnp.bfloat16
@@ -54,17 +56,20 @@
 
 
 def kernel(
+    ndp,
     tok_h, cot_h, src, tgt,
     ag1, ash1, qb1, ob1, mg1, msh1, fb1, pb1, mb1, kvb1,
     wqkv_h, wout_h, wfc_h, wproj_h, emb, midw_h, kvw_h,
-    hid_h, gtok_h, gpre,
+    hid_h, gtok_h, gfull, hidden_o,
     wqkv, wout, wfc, wproj,
     tok2, cot2, xn, qm, kx, kT, vx, vT, es, ep, dsp, ot, oTo, oTf,
     mid, yacc, dxacc, dqT, kb, dbias,
-    pkT, pvbd, pvT, linv, deltap,
+    pkT, pvbd, pvT, linv, deltap, gown, rs, red,
     ag, ash, qb, ob, mg, msh, fb, pb, kvb,
     wsem, lsem, far_s, far_r, xn_s, xn_r, o_s, o_r, d_s, d_r, g_s, g_r, out_s, out_r, loc_out,
+    p1_s, p1_r, pb_s, pb_r, p2_s, p2_r,
 ):
+    dp = lax.axis_index("dp")
     s = lax.axis_index("seq")
     y = lax.div(s, 2)
     c = lax.rem(s, 2)
@@ -94,7 +99,15 @@
     barrier = pltpu.get_barrier_semaphore()
     for peer in (sib, far):
         pl.semaphore_signal(barrier, inc=1, device_id={"seq": peer}, device_id_type=MESH)
-    pl.semaphore_wait(barrier, 2)
+
+    def greet(j, carry):
+        @pl.when(j != dp)
+        def _():
+            pl.semaphore_signal(barrier, inc=1, device_id={"dp": j}, device_id_type=MESH)
+        return carry
+
+    lax.fori_loop(0, ndp, greet, 0)
+    pl.semaphore_wait(barrier, ndp + 1)
 
     def remote(src_ref, dst_ref, ss, rs, peer):
         return pltpu.make_async_remote_copy(
@@ -143,6 +156,7 @@
     pre = mm(embp[:, 0:512], vT[:, 0:512]) + mm(embp[:, 512:1024], vT[:, 512:1024])
     pre = pre + mb1[...].astype(f32).reshape(1, 512)
     hidden = jnp.tanh(pre)
+    hidden_o[...] = hidden
     ld_kvk.wait()
     ld_kvv.wait()
     h3 = jnp.concatenate(split3(hidden), axis=0)
@@ -362,10 +376,77 @@
                 h = 4 * n + 2 * p
                 v = t[h * PP : (h + 1) * PP, 2 * p * 128 : (2 * p + 1) * 128]
                 v = v + t[(h + 1) * PP : (h + 2) * PP, (2 * p + 1) * 128 : (2 * p + 2) * 128]
-                gpre[:, at + h * HD : at + h * HD + 128] = v
+                gown[at + h // 2] = v
 
     prefix_grad(dsp[...], qm, 0)
-    prefix_grad(ep[...], wproj, OWN)
+    prefix_grad(ep[...], wproj, NRED // 2)
+
+    def across(src_ref, dst_ref, ss, rsm, j):
+        return pltpu.make_async_remote_copy(
+            src_ref=src_ref, dst_ref=dst_ref, send_sem=ss, recv_sem=rsm, device_id={"dp": j}, device_id_type=MESH
+        )
+
+    def others(n, fn):
+        def step(j, carry):
+            @pl.when(j != dp)
+            def _():
+                fn(j)
+            return carry
+
+        lax.fori_loop(0, n, step, 0)
+
+    mychunk = c * NRED + dp
+
+    def p1_copy(j):
+        return across(gown.at[j], rs.at[dp], p1_s.at[j], p1_r.at[dp], j)
+
+    def p1_back(j):
+        return across(gown.at[0], rs.at[j], p1_s.at[0], p1_r.at[j], j)
+
+    def p2_copy(j):
+        return across(gfull.at[mychunk], gfull.at[mychunk], p2_s.at[j], p2_r.at[dp], j)
+
+    def p2_back(j):
+        return across(gfull.at[0], gfull.at[c * NRED + j], p2_s.at[0], p2_r.at[j], j)
+
+    def pb_copy():
+        return remote(red.at[0], red.at[1], pb_s.at[0], pb_r.at[0], far)
+
+    def pc_copy():
+        mine = gfull.at[pl.ds(c * NRED, NRED)]
+        return remote(mine, mine, pb_s.at[1], pb_r.at[1], sib)
+
+    def prefix_sum(stage):
+        if stage == 0:
+            others(NRED, lambda j: p1_copy(j).start())
+
+            @pl.when(dp < NRED)
+            def _():
+                rs[dp] = gown[dp]
+        elif stage == 1:
+            @pl.when(dp < NRED)
+            def _():
+                others(ndp, lambda j: p1_back(j).wait_recv())
+                red[0] = lax.fori_loop(1, ndp, lambda j, a: a + rs[j], rs[0])
+                pb_copy().start()
+        elif stage == 2:
+            @pl.when(dp < NRED)
+            def _():
+                pb_copy().wait()
+                gfull[mychunk] = red[0] + red[1]
+                others(ndp, lambda j: p2_copy(j).start())
+        elif stage == 3:
+            others(NRED, lambda j: p2_back(j).wait_recv())
+            pc_copy().start()
+        else:
+            pc_copy().wait()
+            others(NRED, lambda j: p1_copy(j).wait_send())
+
+            @pl.when(dp < NRED)
+            def _():
+                others(ndp, lambda j: p2_copy(j).wait_send())
+
+    prefix_sum(0)
 
     def at_tile(i, j):
         qi = jnp.where(y == 1, j, 3 - i)
@@ -460,9 +541,12 @@
     for i in range(4):
         lax.fori_loop(i, 4, lambda j, carry, i=i: (tile(i, j), carry)[1], 0)
         done_block(i)
+        if i < 3:
+            prefix_sum(i + 1)
         if i:
             finish(i - 1)
     finish(3)
+    prefix_sum(4)
 
     for i in range(2):
         pltpu.make_async_copy(
@@ -473,7 +557,7 @@
     hid_cp.wait_recv()
 
 
-def layer(args):
+def layer(args, ndp):
     vm = pl.BlockSpec(memory_space=pltpu.VMEM)
     hb = pl.BlockSpec(memory_space=pl.ANY)
     sm = pl.BlockSpec(memory_space=pltpu.SMEM)
@@ -483,14 +567,15 @@
     V = pltpu.VMEM
     dma = pltpu.SemaphoreType.DMA
     return pl.pallas_call(
-        kernel,
+        functools.partial(kernel, ndp),
         out_shape=(
             jax.ShapeDtypeStruct(tokens.shape, bf16),
             jax.ShapeDtypeStruct(tokens.shape, bf16),
-            jax.ShapeDtypeStruct((PP, D), f32),
+            jax.ShapeDtypeStruct((2 * NRED, PP, 128), f32),
+            jax.ShapeDtypeStruct((PP, 512), f32),
         ),
         in_specs=[hb, hb, sm, sm] + [vm] * 10 + [hb] * 4 + [vm, hb, hb],
-        out_specs=(hb, hb, vm),
+        out_specs=(hb, hb, vm, vm),
         scratch_shapes=[
             V((D, 3 * D), bf16), V((D, D), bf16), V((D, FF), bf16), V((FF, D), bf16),
             V((OWN, D), bf16), V((OWN, D), bf16), V((D, D), bf16), V((D, D), bf16),
@@ -501,10 +586,12 @@
             V((OWN, D), f32), V((PP + D, 128), f32), V((SEG, SEG), f32),
             V((OWN, NH * PP), bf16), V((NH * PP, OWN), bf16), V((OWN, NH * PP), bf16),
             V((NH, D), f32), V((NH, D), f32),
+            V((NRED, PP, 128), f32), V((ndp, PP, 128), f32), V((2, PP, 128), f32),
             V((1, D), f32), V((1, D), f32), V((1, 3 * D), f32), V((1, D), f32), V((1, D), f32), V((1, D), f32),
             V((1, FF), f32), V((1, D), f32), V((1, 2 * D), f32),
             dma((10,)), dma((1,)), dma((5,)), dma((5,)), dma((5,)), dma((5,)), dma((2,)), dma((2,)),
             dma((2,)), dma((2,)), dma((2,)), dma((2,)), dma((2,)), dma((2,)), dma((2,)),
+            dma((NRED,)), dma((ndp,)), dma((2,)), dma((2,)), dma((ndp,)), dma((NRED,)),
         ],
         compiler_params=pltpu.CompilerParams(
             collective_id=0, has_side_effects=True, vmem_limit_bytes=64 << 20
@@ -513,34 +600,75 @@
       proj_bias, mid_bias, kv_bias, qkv_weight, out_weight, fc_weight, proj_weight, embed_rows, mid_weight, kv_weight)
 
 
-def reparam_back(grad_prefix, embed_f, midw_f, kvw_f, prefix_hidden):
-    grad_kvb = jnp.sum(grad_prefix, axis=0)
-    grad_kvw = jnp.dot(prefix_hidden.T, grad_prefix, precision=HIGH)
-    grad_pre = jnp.dot(grad_prefix, kvw_f.T, precision=HIGH) * (1.0 - prefix_hidden * prefix_hidden)
-    grad_midb = jnp.sum(grad_pre, axis=0)
-    grad_midw = jnp.dot(embed_f.T, grad_pre, precision=HIGH)
-    grad_embed = jnp.dot(grad_pre, midw_f.T, precision=HIGH)
-    return (grad_embed, grad_midw, grad_midb, grad_kvw, grad_kvb)
-
-
-def on_device(*args):
-    embed_rows, mid_weight, mid_bias, kv_weight, kv_bias = args[16:]
-    hidden_out, grad_tokens, own = layer(args)
-    own = own[:PRE]
-    half = lax.rem(lax.axis_index("seq"), 2)
-    parts = jnp.where(jnp.arange(2)[None, None, :, None] == half, own.reshape(PRE, 2, 1, OWN), 0.0)
-    grad_prefix = lax.psum(parts.reshape(PRE, 2 * D), ("dp", "seq"))
-    embed_f = embed_rows.astype(f32)
-    midw_f = mid_weight.astype(f32)
-    kvw_f = kv_weight.astype(f32)
-    prefix_hidden = jnp.tanh(jnp.dot(embed_f, midw_f, precision=HIGH) + mid_bias.astype(f32))
-    return (hidden_out, grad_tokens) + reparam_back(grad_prefix, embed_f, midw_f, kvw_f, prefix_hidden)
+def reparam_kernel(
+    hid_i, gtok_i, gfull, hidden, emb, midw_h, kvw_h,
+    hid_o, gtok_o, gemb, gmidw_o, gmidb, gkvw_o, gkvb,
+    midw, kvw, gkvw, gmidw, sem,
+):
+    def go(i, a, b):
+        cp = pltpu.make_async_copy(a, b, sem.at[i])
+        cp.start()
+        return cp
+
+    ld_kv = go(0, kvw_h, kvw)
+    ld_mid = go(1, midw_h, midw)
+    moves = [go(2, hid_i, hid_o), go(3, gtok_i, gtok_o)]
+    quarter = NRED // 2
+    order = [half * NRED + part * quarter + j for part in (0, 1) for half in (0, 1) for j in range(quarter)]
+    grad = jnp.concatenate([gfull[i] for i in order], axis=1)
+    hid = hidden[...]
+    h0, h1, h2 = split3(hid)
+    g0, g1, g2 = split3(grad)
+    left = jnp.concatenate([h0, h1, h0, h1, h2, h0], axis=0)
+    right = jnp.concatenate([g0, g0, g1, g1, g0, g2], axis=0)
+    W = 512
+    for n in range(2 * D // W):
+        gkvw[:, n * W : (n + 1) * W] = mm(left, right[:, n * W : (n + 1) * W], 0, 0)
+        moves.append(go(4 + n, gkvw.at[:, pl.ds(n * W, W)], gkvw_o.at[:, pl.ds(n * W, W)]))
+    gkvb[...] = jnp.sum(grad, axis=0, keepdims=True).reshape(2 * D)
+    ld_kv.wait()
+    three = mm(jnp.concatenate([g0, g1, g2], axis=0), kvw[...], 1, 1)
+    gp = (three[0:PP] + three[PP : 2 * PP] + three[2 * PP :]) * (1.0 - hid * hid)
+    gmidb[...] = jnp.sum(gp, axis=0, keepdims=True).reshape(512)
+    p0, p1, p2 = split3(gp)
+    p3 = jnp.concatenate([p0, p1, p2], axis=0)
+    embp = jnp.concatenate([emb[...], jnp.zeros((PP - PRE, D), bf16)], axis=0)
+    emb3 = jnp.concatenate([embp] * 3, axis=0)
+    gmidw[...] = mm(emb3, p3, 0, 0)
+    moves.append(go(8, gmidw, gmidw_o))
+    ld_mid.wait()
+    back = mm(p3, midw[...], 1, 1)
+    gemb[...] = (back[0:PP] + back[PP : 2 * PP] + back[2 * PP :])[0:PRE]
+    for cp in moves:
+        cp.wait()
+
+
+def on_device(ndp, *args):
+    embed_rows, mid_weight, _, kv_weight, _ = args[16:]
+    hidden_out, grad_tokens, gfull, hidden = layer(args, ndp)
+    vm = pl.BlockSpec(memory_space=pltpu.VMEM)
+    hb = pl.BlockSpec(memory_space=pl.ANY)
+    sds = jax.ShapeDtypeStruct
+    return pl.pallas_call(
+        reparam_kernel,
+        out_shape=(
+            sds(hidden_out.shape, bf16), sds(grad_tokens.shape, bf16), sds((PRE, D), f32), sds((D, 512), f32),
+            sds((512,), f32), sds((512, 2 * D), f32), sds((2 * D,), f32),
+        ),
+        in_specs=[hb, hb, vm, vm, vm, hb, hb],
+        out_specs=(hb, hb, vm, hb, vm, hb, vm),
+        scratch_shapes=[
+            pltpu.VMEM((D, 512), bf16), pltpu.VMEM((512, 2 * D), bf16), pltpu.VMEM((512, 2 * D), f32),
+            pltpu.VMEM((D, 512), f32), pltpu.SemaphoreType.DMA((9,)),
+        ],
+        compiler_params=pltpu.CompilerParams(vmem_limit_bytes=32 << 20),
+    )(hidden_out, grad_tokens, gfull, hidden, embed_rows, mid_weight, kv_weight)
 
 
 def solution(mesh):
     split = P("dp", "seq", None)
     return jax.shard_map(
-        on_device,
+        functools.partial(on_device, mesh.shape["dp"]),
         mesh=mesh,
         in_specs=(split, split, P("dp"), P("dp")) + (P(),) * 17,
         out_specs=(split, split, P(), P(), P(), P(), P()),

time: 270 us -> 119 us (0.44)
  waiting for transfers between devices: 123 us -> 0 us
  between operations: 14.3 us -> 0.84 us
  matrix products: 13.1 us -> 0 us
  local copies, waits for them, and re-layouts: 4.85 us -> 7.68 us
    psum x1 -> x0, waiting for transfers between devices: 123 us -> none  [on_device(): grad_prefix = lax.psum(parts.reshape(PRE, 2 * D), ('dp', 'seq'))]
    dot_general x5 -> x0, matrix products: 13.1 us -> none  [the longest x1 5.01 us: reparam_back(): grad_kvw = jnp.dot(prefix_hidden.T, grad_prefix, precision=HIGH)]
    unnamed x13 -> x14, local copies, waits for them, and re-layouts: 3.78 us -> 7.68 us
    pallas_call x1 -> x2, Pallas kernels: 109 us -> 108 us  [the longest x1 104 us: layer(): pl.pallas_call(functools.partial(kernel, ndp), out_shape=(jax.ShapeDtypeS...]
  transfers between devices with their start and end apart: 1 -> 0, of which waited for: 1 -> 0; matrix products, arithmetic and copies ran while one was open for 1% -> 0% of each run, Pallas kernels for 0% -> 0%
where the time goes in v2:
time: 119 us; the launch traced here: 117 us
  Pallas kernels  108 us (91%)
  local copies, waits for them, and re-layouts  7.68 us (6%)
    pallas_call x1, Pallas kernels, layer(): pl.pallas_call(functools.partial(kernel, ndp), out_shape=(jax.ShapeDtypeS...  104 us
    unnamed x14, local copies, waits for them, and re-layouts  7.68 us
    pallas_call x1, Pallas kernels, on_device(): pl.pallas_call(reparam_kernel, out_shape=(sds(hidden_out.shape, bf16), sd...  4.26 us

profile of v2, /device:TPU:0, one launch (start us, length us, event | category | flops | bytes accessed | tf_op | source)
XLA Modules:
  0.0 116.7 jit_solution(7549987515481368995)
XLA Ops:
  0.6 103.9 %shard_map.252 = (bf16[2,256,1024]{2,1,0:T(8,128)(2,1)}, bf16[2,256,1024]{2,1,0:T(8,128)(2,1)}, f32[16,16,128]{2,1,0:T(8,128)}, f32[16,512]{1,0:T(8,128)}) custom-call(bf16[2,256,1024]{2,1,0:T(8,128)(2,1)} %tok_h.1, bf16[2,256,1024]{2,1,0:T(8,128)(2,1)} %cot_h.1, s32[2]{0:T(128)} %src.1, s32[2]{0:T(128)} %tgt.1, bf16[1024]{0:T(1024)(128)(2,1)} %ag1.1, ...), custom_call_target="tpu_custom_call" | custom-call | tf_op jit(solution)/shard_map/pallas_call | solution.py:569
  104.5 0.0 copy-start
  104.5 1.6 %copy-done = bf16[512,2048]{1,0:T(8,128)(2,1)S(1)} copy-done((bf16[512,2048]{1,0:T(8,128)(2,1)S(1)}, bf16[512,2048]{1,0:T(8,128)(2,1)}, u32[]{:S(2)}) %copy-start) | copy-done | bytes 2097176
  106.1 0.0 copy-start.1
  106.1 1.2 %copy-done.1 = bf16[1024,512]{1,0:T(8,128)(2,1)S(1)} copy-done((bf16[1024,512]{1,0:T(8,128)(2,1)S(1)}, bf16[1024,512]{1,0:T(8,128)(2,1)}, u32[]{:S(2)}) %copy-start.1) | copy-done | bytes 1048600
  107.3 0.0 copy-start.2
  107.4 1.2 %copy-done.2 = bf16[2,256,1024]{2,1,0:T(8,128)(2,1)S(1)} copy-done((bf16[2,256,1024]{2,1,0:T(8,128)(2,1)S(1)}, bf16[2,256,1024]{2,1,0:T(8,128)(2,1)}, u32[]{:S(2)}) %copy-start.2) | copy-done | bytes 1048600
  108.6 0.0 copy-start.3
  108.6 1.2 %copy-done.3 = bf16[2,256,1024]{2,1,0:T(8,128)(2,1)S(1)} copy-done((bf16[2,256,1024]{2,1,0:T(8,128)(2,1)S(1)}, bf16[2,256,1024]{2,1,0:T(8,128)(2,1)}, u32[]{:S(2)}) %copy-start.3) | copy-done | bytes 1048600
  109.8 0.0 copy-start.4
  109.8 0.9 copy-done.4
  110.7 0.0 copy-start.5
  110.7 0.8 copy-done.5
  111.5 0.0 copy-start.6
  111.5 0.8 copy-done.6
  112.2 4.3 %shard_map.253 = (bf16[2,256,1024]{2,1,0:T(8,128)(2,1)}, bf16[2,256,1024]{2,1,0:T(8,128)(2,1)}, f32[10,1024]{1,0:T(8,128)}, f32[1024,512]{1,0:T(8,128)}, f32[512...) custom-call(bf16[2,256,1024]{2,1,0:T(8,128)(2,1)S(1)} %copy-done.2, bf16[2,256,1024]{2,1,0:T(8,128)(2,1)S(1)} %copy-done.3, ...), custom_call_target="tpu_custom_call" | custom-call | tf_op jit(solution)/shard_map/pallas_call | solution.py:652
Async XLA Ops:
  104.5 1.6 %copy-start = (bf16[512,2048]{1,0:T(8,128)(2,1)S(1)}, bf16[512,2048]{1,0:T(8,128)(2,1)}, u32[]{:S(2)}) copy-start(bf16[512,2048]{1,0:T(8,128)(2,1)} %kvw_h.3) | copy-start | bytes 6291460
  106.1 1.2 %copy-start.1 = (bf16[1024,512]{1,0:T(8,128)(2,1)S(1)}, bf16[1024,512]{1,0:T(8,128)(2,1)}, u32[]{:S(2)}) copy-start(bf16[1024,512]{1,0:T(8,128)(2,1)} %midw_h.3) | copy-start | bytes 3145732
  107.3 1.2 %copy-start.2 = (bf16[2,256,1024]{2,1,0:T(8,128)(2,1)S(1)}, bf16[2,256,1024]{2,1,0:T(8,128)(2,1)}, u32[]{:S(2)}) copy-start(bf16[2,256,1024]{2,1,0:T(8,128)(2,1)} %get-tuple-element.11.hid_i) | copy-start | bytes 3145732
  108.6 1.2 %copy-start.3 = (bf16[2,256,1024]{2,1,0:T(8,128)(2,1)S(1)}, bf16[2,256,1024]{2,1,0:T(8,128)(2,1)}, u32[]{:S(2)}) copy-start(bf16[2,256,1024]{2,1,0:T(8,128)(2,1)} %get-tuple-element.12.gtok_i) | copy-start | bytes 3145732
  109.8 0.9 copy-start.4
  110.7 0.8 copy-start.5
  111.5 0.8 copy-start.6

commit v3 on v2

--- a/solution.py
+++ b/solution.py
@@ -17,6 +17,7 @@
 NH = 8
 NB = 4
 NRED = 8
+VR = 80
 EPS = 1e-05
 NEG = -1e30
 MESH = pl.DeviceIdType.MESH
@@ -64,9 +65,9 @@
     wqkv, wout, wfc, wproj,
     tok2, cot2, xn, qm, kx, kT, vx, vT, es, ep, dsp, ot, oTo, oTf,
     mid, yacc, dxacc, dqT, kb, dbias,
-    pkT, pvbd, pvT, linv, deltap, gown, rs, red,
+    pkT, pvbd, pvT, pc0, pc1, linv, deltap, gown, rs, red,
     ag, ash, qb, ob, mg, msh, fb, pb, kvb,
-    wsem, lsem, far_s, far_r, xn_s, xn_r, o_s, o_r, d_s, d_r, g_s, g_r, out_s, out_r, loc_out,
+    wsem, far_s, far_r, xn_s, xn_r, o_s, o_r, d_s, d_r, g_s, g_r, out_s, out_r, loc_out,
     p1_s, p1_r, pb_s, pb_r, p2_s, p2_r,
 ):
     dp = lax.axis_index("dp")
@@ -86,15 +87,10 @@
         return cp
 
     ld_tok = load(0, tok_h.at[y], tok2.at[pl.ds(0, SEG)])
-    ld_mid0 = load(1, midw_h.at[pl.ds(0, 512)], vT.at[:, pl.ds(0, 512)])
-    ld_mid1 = load(2, midw_h.at[pl.ds(512, 512)], vT.at[:, pl.ds(512, 512)])
+    ld_mid0 = load(1, midw_h.at[pl.ds(0, 512)], vT.at[pl.ds(0, 512), pl.ds(0, 512)])
+    ld_mid1 = load(2, midw_h.at[pl.ds(512, 512)], vT.at[pl.ds(0, 512), pl.ds(512, 512)])
     ld_kvk = load(3, kvw_h.at[:, pl.ds(cw, OWN)], kT.at[:, pl.ds(0, OWN)])
     ld_kvv = load(4, kvw_h.at[:, pl.ds(aligned(D + c * OWN, OWN), OWN)], kT.at[:, pl.ds(OWN, OWN)])
-    ld_qkv = load(5, wqkv_h, wqkv)
-    ld_cot = load(6, cot_h.at[y], cot2.at[pl.ds(0, SEG)])
-    ld_out = load(7, wout_h, wout)
-    ld_fc = load(8, wfc_h, wfc)
-    ld_proj = load(9, wproj_h, wproj)
 
     barrier = pltpu.get_barrier_semaphore()
     for peer in (sib, far):
@@ -126,6 +122,7 @@
     ]
     for cp in tok_cp:
         cp.start()
+    ld_qkv = load(5, wqkv_h, wqkv)
     cot_cp = remote(cot_h.at[1 - y], cot2.at[pl.ds(SEG, SEG)], far_s.at[NCH], far_r.at[NCH], far)
 
     for dst, vec in ((ag, ag1), (ash, ash1), (qb, qb1), (ob, ob1), (mg, mg1), (msh, msh1), (fb, fb1), (pb, pb1), (kvb, kvb1)):
@@ -149,11 +146,13 @@
     xl = xn.at[pl.ds(aligned(bl * SEG, SEG), SEG)]
     xl_cp = remote(xl, xl, xn_s.at[NCH], xn_r.at[NCH], sib)
     xl_cp.start()
+    ld_cot = load(6, cot_h.at[y], cot2.at[pl.ds(0, SEG)])
+    ld_out = load(7, wout_h, wout)
 
     ld_mid0.wait()
     ld_mid1.wait()
     embp = jnp.concatenate([emb[...], jnp.zeros((PP - PRE, D), bf16)], axis=0)
-    pre = mm(embp[:, 0:512], vT[:, 0:512]) + mm(embp[:, 512:1024], vT[:, 512:1024])
+    pre = mm(embp[:, 0:512], vT[0:512, 0:512]) + mm(embp[:, 512:1024], vT[0:512, 512:1024])
     pre = pre + mb1[...].astype(f32).reshape(1, 512)
     hidden = jnp.tanh(pre)
     hidden_o[...] = hidden
@@ -172,7 +171,14 @@
     pv8 = jnp.where(hr == hc, jnp.concatenate([pv] * NH, axis=0), 0.0)
     pvbd[...] = pv8.astype(bf16)
     pkT[...] = pk8.T.astype(bf16)
-    pvT[...] = pv8.T.astype(bf16)
+    one_t = jnp.where(lax.broadcasted_iota(jnp.int32, (VR - HD, D), 0) == 0, 1.0, 0.0).astype(bf16)
+    pv_t = pv8.T
+    up = lax.broadcasted_iota(jnp.int32, (VR - HD, NH * PP), 0)
+    for h in range(NH):
+        here = lax.broadcasted_iota(jnp.int32, (VR - HD, NH * PP), 1) // PP == h
+        vT[h * VR + HD : (h + 1) * VR, :] = one_t
+        pvT[h * VR : h * VR + HD, :] = pv_t[h * HD : (h + 1) * HD].astype(bf16)
+        pvT[h * VR + HD : (h + 1) * VR, :] = jnp.where(here & (up == 0), 1.0, 0.0).astype(bf16)
 
     lane = lax.broadcasted_iota(jnp.int32, (1, 128), 1)
     lo_half = jnp.where(lane < HD, 1.0, 0.0).astype(bf16)
@@ -195,7 +201,9 @@
         kT[:, rows] = k.T
         vw = pl.ds(aligned(2 * D + c * OWN, OWN), OWN)
         v = (mm(x, wqkv[:, vw]) + qb[:, vw]).astype(bf16)
-        vT[:, rows] = v.T
+        vt = v.T
+        for h in range(NH):
+            vT[h * VR : h * VR + HD, rows] = vt[h * HD : (h + 1) * HD]
         for hp in range(4):
             kx[hp, krows, :] = k[:, hp * 128 : (hp + 1) * 128]
             vx[hp, rows, :] = v[:, hp * 128 : (hp + 1) * 128]
@@ -206,6 +214,7 @@
     project(lax.bitwise_xor(bl, 1))
 
     fw = []
+    ld_ffn = []
     for j in range(NCH):
         tok_cp[j].wait_recv()
         norm_rows(SEG + j * CH, CH, br * SEG + j * CH)
@@ -213,6 +222,12 @@
         cp = remote(xr, xr, xn_s.at[j], xn_r.at[j], sib)
         cp.start()
         fw.append(cp)
+        if j < 2:
+            half = pl.ds(j * OWN, OWN)
+            ld_ffn.append(load(8 + j, wfc_h.at[half], wfc.at[half]))
+        else:
+            half = pl.ds((j - 2) * 2 * D, 2 * D)
+            ld_ffn.append(load(8 + j, wproj_h.at[half], wproj.at[half]))
     for cp in tok_cp:
         cp.wait_send()
     cot_cp.start()
@@ -237,36 +252,48 @@
             oTo.at[b], oTf.at[slot_of(b), pl.ds(cw, OWN)], o_s.at[slot_of(b)], o_r.at[slot_of(b)], sib
         )
 
+    scs = ((yacc, pc0), (dxacc, pc1))
     for b in (3, 2, 1, 0):
         cols = slice(b * SEG, (b + 1) * SEG)
         low = PP + b * SEG
         off = SEG * (b * (b + 1) // 2)
         dbias[...] = jnp.where(tri, twice(kb[low : low + SEG, :]), NEG)
 
-        def heads(hp, carry, b=b, cols=cols, low=low, off=off):
-            for u in range(2):
-                h = 2 * hp + u
-                qh = qm[cols, pl.ds(aligned(h * 128, 128), 128)]
-                s0 = mm(kx[hp, 0:low, :], qh, 1, 1) + twice(kb[0:low, :])
-                s1 = mm(kx[hp, low : low + SEG, :], qh, 1, 1) + dbias[...]
-                m = jnp.maximum(jnp.max(s0, axis=0, keepdims=True), jnp.max(s1, axis=0, keepdims=True))
-                e0 = jnp.exp(s0 - m)
-                e1 = jnp.exp(s1 - m)
-                den = jnp.sum(e0, axis=0, keepdims=True) + jnp.sum(e1, axis=0, keepdims=True)
-                linv[pl.ds(h, 1), cols] = 1.0 / den
-                p0 = e0.astype(bf16)
-                p1 = e1.astype(bf16)
-                ep[pl.ds(aligned(h * PP, PP), PP), cols] = p0[0:PP]
-                hrows = pl.ds(aligned(h * HD, HD), HD)
-                if b:
-                    es[h, off : off + b * SEG, :] = p0[PP:]
-                es[h, off + b * SEG : off + (b + 1) * SEG, :] = p1
-                ot[hrows, :] = mm(vT[hrows, 0 : (b + 1) * SEG], es[h, off : off + (b + 1) * SEG, :])
-            return carry
-
-        lax.fori_loop(0, 4, heads, 0)
-        o = (ot[...] + mm(pvT[...], ep[:, cols])) * rep(linv[:, cols], HD)
-        oTo[b] = o.astype(bf16)
+        width = (b + 1) * SEG
+
+        def stage_a(h):
+            sc, pc = scs[h % 2]
+            qh = qm[cols, h * 128 : (h + 1) * 128]
+            s0 = mm(kx[h // 2, 0:low, :], qh, 1, 1) + twice(kb[0:low, :])
+            pc[...] = s0[0:PP]
+            if b:
+                sc[0 : b * SEG, 0:SEG] = s0[PP:]
+            sc[b * SEG : width, 0:SEG] = mm(kx[h // 2, low : low + SEG, :], qh, 1, 1) + dbias[...]
+
+        def stage_b(h):
+            sc, pc = scs[h % 2]
+            m = jnp.maximum(
+                jnp.max(sc[0:width, 0:SEG], axis=0, keepdims=True), jnp.max(pc[...], axis=0, keepdims=True)
+            )
+            ep[h * PP : (h + 1) * PP, cols] = jnp.exp(pc[...] - m).astype(bf16)
+            es[h, off : off + width, :] = jnp.exp(sc[0:width, 0:SEG] - m).astype(bf16)
+
+        def stage_c(h):
+            ot[h * VR : (h + 1) * VR, :] = mm(vT[h * VR : (h + 1) * VR, 0:width], es[h, off : off + width, :])
+
+        stage_a(0)
+        for h in range(NH):
+            if h + 1 < NH:
+                stage_a(h + 1)
+            if h:
+                stage_c(h - 1)
+            stage_b(h)
+        stage_c(NH - 1)
+        o = ot[...] + mm(pvT[...], ep[:, cols])
+        for h in range(NH):
+            inv = 1.0 / o[h * VR + HD : h * VR + HD + 1]
+            linv[h : h + 1, cols] = inv
+            oTo[b, h * HD : (h + 1) * HD, :] = (o[h * VR : h * VR + HD] * inv).astype(bf16)
 
         @pl.when(c == b % 2)
         def _(b=b):
@@ -299,8 +326,8 @@
     for sl in (0, 1):
         pltpu.make_async_copy(oTo.at[sl], oTo.at[sl], o_s.at[sl]).wait()
 
-    ld_fc.wait()
-    ld_proj.wait()
+    for cp in ld_ffn:
+        cp.wait()
     yacc[...] = jnp.zeros_like(yacc)
     dxacc[...] = jnp.zeros_like(dxacc)
     FC = 512
@@ -458,23 +485,39 @@
         qr = pl.ds(aligned(qi * SEG, SEG), SEG)
         kr = pl.ds(aligned(ki * SEG, SEG), SEG)
         off = pl.ds(aligned((lax.div(qi * (qi + 1), 2) + ki) * SEG, SEG), SEG)
+        sbuf = (dbias, ot.at[pl.ds(0, SEG)])
+        dbuf = [vT.at[pl.ds(0, SEG), pl.ds(n * SEG, SEG)] for n in range(4)]
+
+        def stage_a(h):
+            sbuf[h % 2][...] = mm(vx[h // 2, kr, :], wproj[qr, h * 128 : (h + 1) * 128], 1, 1)
+
+        def stage_b(h):
+            dbuf[h % 4][...] = (
+                es[h, off, :].astype(f32) * (sbuf[h % 2][...] - deltap[h : h + 1, qr])
+            ).astype(bf16)
+
+        def stage_c(hp):
+            hl = slice(hp * 128, (hp + 1) * 128)
+            h = 2 * hp
+            w0 = slice(h * 128, (h + 1) * 128)
+            w1 = slice((h + 1) * 128, (h + 2) * 128)
+            d0, d1 = dbuf[h % 4], dbuf[(h + 1) % 4]
+            dk[kr, hl] += mm(d0[...], qm[qr, w0]) + mm(d1[...], qm[qr, w1])
+            dv[kr, hl] += mm(es[h, off, :], wproj[qr, w0]) + mm(es[h + 1, off, :], wproj[qr, w1])
+            for hh, d in ((h, d0), (h + 1, d1)):
+                hrows = slice(hh * HD, (hh + 1) * HD)
+                dqT[hrows, qr] += mm(kT[hrows, kr], d[...])
+
+        stage_a(0)
         for hp in range(4):
-            hl = slice(hp * 128, (hp + 1) * 128)
-            gk = dk[kr, hl]
-            gv = dv[kr, hl]
-            for u in range(2):
-                h = 2 * hp + u
-                hw = slice(h * 128, (h + 1) * 128)
-                hrows = slice(h * HD, (h + 1) * HD)
-                doh = wproj[qr, hw]
-                e = es[h, off, :]
-                dp = mm(vx[hp, kr, :], doh, 1, 1)
-                ds = (e.astype(f32) * (dp - deltap[h : h + 1, qr])).astype(bf16)
-                gv = gv + mm(e, doh)
-                gk = gk + mm(ds, qm[qr, hw])
-                dqT[hrows, qr] += mm(kT[hrows, kr], ds)
-            dk[kr, hl] = gk
-            dv[kr, hl] = gv
+            stage_a(2 * hp + 1)
+            stage_b(2 * hp)
+            if hp < 3:
+                stage_a(2 * hp + 2)
+            stage_b(2 * hp + 1)
+            if hp:
+                stage_c(hp - 1)
+        stage_c(3)
 
     def block_at(i):
         return jnp.where(y == 1, i, 3 - i)
@@ -484,7 +527,7 @@
         return remote(
             wfc.at[pl.ds(aligned(sl * SEG, SEG), SEG), pl.ds(2048, 1536)],
             wfc.at[pl.ds(aligned((2 * sl + c) * SEG, SEG), SEG), pl.ds(0, 1536)],
-            g_s.at[i // 2], g_r.at[i // 2], sib,
+            g_s.at[lax.div(i, 2)], g_r.at[lax.div(i, 2)], sib,
         )
 
     def done_block(i):
@@ -523,10 +566,23 @@
             rows2 = pl.ds(aligned(OWN + sl * SEG, SEG), SEG)
             gm = jnp.concatenate([dxacc[rows, :], dxacc[rows2, :]], axis=1)
             res = gm + norm_back(tok2[rows, :].astype(f32), acc * ag[...])
+
+            @pl.when(i < 2)
+            def _():
+                hid_cp.wait_send()
+
+            @pl.when(i >= 2)
+            def _():
+                hid_lo.wait()
+
             xn[rows, :] = res.astype(bf16)
-            if i < 2:
+
+            @pl.when(i < 2)
+            def _():
                 gt_cp().start()
-            else:
+
+            @pl.when(i >= 2)
+            def _():
                 gt_lo().start()
 
     def gt_cp():
@@ -535,17 +591,25 @@
     def gt_lo():
         return pltpu.make_async_copy(xn.at[pl.ds(0, SEG)], gtok_h.at[y], loc_out.at[1])
 
-    hid_cp.wait_send()
-    hid_lo.wait()
     cot_cp.wait_send()
-    for i in range(4):
-        lax.fori_loop(i, 4, lambda j, carry, i=i: (tile(i, j), carry)[1], 0)
-        done_block(i)
-        if i < 3:
-            prefix_sum(i + 1)
-        if i:
+    def round_of(i, carry):
+        lax.fori_loop(i, 4, lambda j, cc: (tile(i, j), cc)[1], 0)
+
+        @pl.when(i < 4)
+        def _():
+            done_block(i)
+
+        for k in range(3):
+            @pl.when(i == k)
+            def _(k=k):
+                prefix_sum(k + 1)
+
+        @pl.when(i > 0)
+        def _():
             finish(i - 1)
-    finish(3)
+        return carry
+
+    lax.fori_loop(0, 5, round_of, 0)
     prefix_sum(4)
 
     for i in range(2):
@@ -579,17 +643,18 @@
         scratch_shapes=[
             V((D, 3 * D), bf16), V((D, D), bf16), V((D, FF), bf16), V((FF, D), bf16),
             V((OWN, D), bf16), V((OWN, D), bf16), V((D, D), bf16), V((D, D), bf16),
-            V((4, PP + D, 128), bf16), V((OWN, D), bf16), V((4, D, 128), bf16), V((OWN, D), bf16),
+            V((4, PP + D, 128), bf16), V((OWN, D), bf16), V((4, D, 128), bf16), V((NH * VR, D), bf16),
             V((NH, 10 * SEG, SEG), bf16), V((NH * PP, D), bf16), V((NH * PP, D), bf16),
-            V((OWN, SEG), f32), V((NB, OWN, SEG), bf16), V((2, D, SEG), bf16),
+            V((NH * VR, SEG), f32), V((NB, OWN, SEG), bf16), V((2, D, SEG), bf16),
             V((D, OWN), f32), V((D, OWN), f32), V((D, OWN), f32),
             V((OWN, D), f32), V((PP + D, 128), f32), V((SEG, SEG), f32),
-            V((OWN, NH * PP), bf16), V((NH * PP, OWN), bf16), V((OWN, NH * PP), bf16),
+            V((OWN, NH * PP), bf16), V((NH * PP, OWN), bf16), V((NH * VR, NH * PP), bf16),
+            V((PP, SEG), f32), V((PP, SEG), f32),
             V((NH, D), f32), V((NH, D), f32),
             V((NRED, PP, 128), f32), V((ndp, PP, 128), f32), V((2, PP, 128), f32),
             V((1, D), f32), V((1, D), f32), V((1, 3 * D), f32), V((1, D), f32), V((1, D), f32), V((1, D), f32),
             V((1, FF), f32), V((1, D), f32), V((1, 2 * D), f32),
-            dma((10,)), dma((1,)), dma((5,)), dma((5,)), dma((5,)), dma((5,)), dma((2,)), dma((2,)),
+            dma((12,)), dma((5,)), dma((5,)), dma((5,)), dma((5,)), dma((2,)), dma((2,)),
             dma((2,)), dma((2,)), dma((2,)), dma((2,)), dma((2,)), dma((2,)), dma((2,)),
             dma((NRED,)), dma((ndp,)), dma((2,)), dma((2,)), dma((ndp,)), dma((NRED,)),
         ],
@@ -603,16 +668,17 @@
 def reparam_kernel(
     hid_i, gtok_i, gfull, hidden, emb, midw_h, kvw_h,
     hid_o, gtok_o, gemb, gmidw_o, gmidb, gkvw_o, gkvb,
-    midw, kvw, gkvw, gmidw, sem,
+    midw, kvw, gkvw, gmidw, hid_v, gtok_v, sem,
 ):
     def go(i, a, b):
         cp = pltpu.make_async_copy(a, b, sem.at[i])
         cp.start()
         return cp
 
+    ld_out = [go(2, hid_i, hid_v), go(3, gtok_i, gtok_v)]
     ld_kv = go(0, kvw_h, kvw)
     ld_mid = go(1, midw_h, midw)
-    moves = [go(2, hid_i, hid_o), go(3, gtok_i, gtok_o)]
+    moves = []
     quarter = NRED // 2
     order = [half * NRED + part * quarter + j for part in (0, 1) for half in (0, 1) for j in range(quarter)]
     grad = jnp.concatenate([gfull[i] for i in order], axis=1)
@@ -625,6 +691,9 @@
     for n in range(2 * D // W):
         gkvw[:, n * W : (n + 1) * W] = mm(left, right[:, n * W : (n + 1) * W], 0, 0)
         moves.append(go(4 + n, gkvw.at[:, pl.ds(n * W, W)], gkvw_o.at[:, pl.ds(n * W, W)]))
+    for cp in ld_out:
+        cp.wait()
+    moves += [go(9, hid_v, hid_o), go(10, gtok_v, gtok_o)]
     gkvb[...] = jnp.sum(grad, axis=0, keepdims=True).reshape(2 * D)
     ld_kv.wait()
     three = mm(jnp.concatenate([g0, g1, g2], axis=0), kvw[...], 1, 1)
@@ -659,9 +728,10 @@
         out_specs=(hb, hb, vm, hb, vm, hb, vm),
         scratch_shapes=[
             pltpu.VMEM((D, 512), bf16), pltpu.VMEM((512, 2 * D), bf16), pltpu.VMEM((512, 2 * D), f32),
-            pltpu.VMEM((D, 512), f32), pltpu.SemaphoreType.DMA((9,)),
+            pltpu.VMEM((D, 512), f32), pltpu.VMEM(hidden_out.shape, bf16), pltpu.VMEM(hidden_out.shape, bf16),
+            pltpu.SemaphoreType.DMA((11,)),
         ],
-        compiler_params=pltpu.CompilerParams(vmem_limit_bytes=32 << 20),
+        compiler_params=pltpu.CompilerParams(vmem_limit_bytes=64 << 20),
     )(hidden_out, grad_tokens, gfull, hidden, embed_rows, mid_weight, kv_weight)
 
 

time: 119 us -> 96.9 us (0.81)
  Pallas kernels: 108 us -> 94.7 us
  local copies, waits for them, and re-layouts: 7.68 us -> 0 us
    pallas_call x1, Pallas kernels: 104 us -> 86.2 us  [layer(): pl.pallas_call(functools.partial(kernel, ndp), out_shape=(jax.ShapeDtypeS...]
    unnamed x14 -> x0, local copies, waits for them, and re-layouts: 7.68 us -> none
    pallas_call x1, Pallas kernels: 4.26 us -> 8.57 us  [on_device(): pl.pallas_call(reparam_kernel, out_shape=(sds(hidden_out.shape, bf16), sd...]
where the time goes in v3:
time: 96.9 us; the launch traced here: 95.6 us
  Pallas kernels  94.7 us (98%)
    pallas_call x1, Pallas kernels, layer(): pl.pallas_call(functools.partial(kernel, ndp), out_shape=(jax.ShapeDtypeS...  86.2 us
    pallas_call x1, Pallas kernels, on_device(): pl.pallas_call(reparam_kernel, out_shape=(sds(hidden_out.shape, bf16), sd...  8.57 us

profile of v3, /device:TPU:0, one launch (start us, length us, event | category | flops | bytes accessed | tf_op | source)
XLA Modules:
  0.0 95.6 jit_solution(14592293424337136595)
XLA Ops:
  0.6 86.2 %shard_map.252 = (bf16[2,256,1024]{2,1,0:T(8,128)(2,1)}, bf16[2,256,1024]{2,1,0:T(8,128)(2,1)}, f32[16,16,128]{2,1,0:T(8,128)}, f32[16,512]{1,0:T(8,128)}) custom-call(bf16[2,256,1024]{2,1,0:T(8,128)(2,1)} %tok_h.1, bf16[2,256,1024]{2,1,0:T(8,128)(2,1)} %cot_h.1, s32[2]{0:T(128)} %src.1, s32[2]{0:T(128)} %tgt.1, bf16[1024]{0:T(1024)(128)(2,1)} %ag1.1, ...), custom_call_target="tpu_custom_call" | custom-call | tf_op jit(solution)/shard_map/pallas_call | solution.py:633
  86.8 8.6 %shard_map.253 = (bf16[2,256,1024]{2,1,0:T(8,128)(2,1)}, bf16[2,256,1024]{2,1,0:T(8,128)(2,1)}, f32[10,1024]{1,0:T(8,128)}, f32[1024,512]{1,0:T(8,128)}, f32[512...) custom-call(bf16[2,256,1024]{2,1,0:T(8,128)(2,1)} %get-tuple-element.11.hid_i, ...), custom_call_target="tpu_custom_call" | custom-call | tf_op jit(solution)/shard_map/pallas_call | solution.py:721

commit v4 on v3

--- a/solution.py
+++ b/solution.py
@@ -217,6 +217,8 @@
     ld_ffn = []
     for j in range(NCH):
         tok_cp[j].wait_recv()
+        if j == NCH - 2:
+            cot_cp.start()
         norm_rows(SEG + j * CH, CH, br * SEG + j * CH)
         xr = xn.at[pl.ds(aligned(br * SEG + j * CH, CH), CH)]
         cp = remote(xr, xr, xn_s.at[j], xn_r.at[j], sib)
@@ -230,7 +232,6 @@
             ld_ffn.append(load(8 + j, wproj_h.at[half], wproj.at[half]))
     for cp in tok_cp:
         cp.wait_send()
-    cot_cp.start()
     project(br)
     for cp in fw:
         cp.wait()

time: 96.9 us -> 96.9 us (level); the launches traced: 95.6 us -> 96.7 us
  Pallas kernels: 94.7 us -> 95.9 us
    pallas_call x1, Pallas kernels: 86.2 us -> 87.3 us  [layer(): pl.pallas_call(functools.partial(kernel, ndp), out_shape=(jax.ShapeDtypeS...]
where the time goes in v4:
time: 96.9 us; the launch traced here: 96.7 us
  Pallas kernels  95.9 us (99%)
    pallas_call x1, Pallas kernels, layer(): pl.pallas_call(functools.partial(kernel, ndp), out_shape=(jax.ShapeDtypeS...  87.3 us
    pallas_call x1, Pallas kernels, on_device(): pl.pallas_call(reparam_kernel, out_shape=(sds(hidden_out.shape, bf16), sd...  8.57 us

profile of v4, /device:TPU:0, one launch (start us, length us, event | category | flops | bytes accessed | tf_op | source)
XLA Modules:
  0.0 96.7 jit_solution(17350379247721182080)
XLA Ops:
  0.6 87.3 %shard_map.252 = (bf16[2,256,1024]{2,1,0:T(8,128)(2,1)}, bf16[2,256,1024]{2,1,0:T(8,128)(2,1)}, f32[16,16,128]{2,1,0:T(8,128)}, f32[16,512]{1,0:T(8,128)}) custom-call(bf16[2,256,1024]{2,1,0:T(8,128)(2,1)} %tok_h.1, bf16[2,256,1024]{2,1,0:T(8,128)(2,1)} %cot_h.1, s32[2]{0:T(128)} %src.1, s32[2]{0:T(128)} %tgt.1, bf16[1024]{0:T(1024)(128)(2,1)} %ag1.1, ...), custom_call_target="tpu_custom_call" | custom-call | tf_op jit(solution)/shard_map/pallas_call | solution.py:634
  88.0 8.6 %shard_map.253 = (bf16[2,256,1024]{2,1,0:T(8,128)(2,1)}, bf16[2,256,1024]{2,1,0:T(8,128)(2,1)}, f32[10,1024]{1,0:T(8,128)}, f32[1024,512]{1,0:T(8,128)}, f32[512...) custom-call(bf16[2,256,1024]{2,1,0:T(8,128)(2,1)} %get-tuple-element.11.hid_i, ...), custom_call_target="tpu_custom_call" | custom-call | tf_op jit(solution)/shard_map/pallas_call | solution.py:722
